TPU v7x, 32 devices: a whole 2x2x4 slice. The times are simulated.
32 devices in a mesh: seq: 8 (over y, x, core), dp: 4 (over z).
Axes of the slice: x: 2, y: 2, z: 4, core: 2. Of those that a mesh axis runs over, the one named last changes fastest.
Arguments:
- tokens: bfloat16 [12, 1024, 1024], P('dp', 'seq'), may hold values from -6 to 6
- first_values: bfloat16 [12, 1024, 1024], P('dp', 'seq'), may hold values from -6 to 6
- out_grad: bfloat16 [12, 1024, 1024], P('dp', 'seq'), may hold values from -6 to 6
- lengths: int32 [12], P('dp'), may hold values from 1 to 1024, as said below
- norm1_gain: bfloat16 [1024], P(('seq', 'dp')), may hold values from 0.099609375 to 1.8984375
- qkv_weight: bfloat16 [1024, 3072], P(('seq', 'dp')), may hold values from -0.1875 to 0.1875
- out_weight: bfloat16 [1024, 1024], P(('seq', 'dp')), may hold values from -1.5 to 1.5
- norm2_gain: bfloat16 [1024], P(('seq', 'dp')), may hold values from 0.099609375 to 1.8984375
- gate_weight: bfloat16 [1024, 2816], P(('seq', 'dp')), may hold values from -0.1875 to 0.1875
- up_weight: bfloat16 [1024, 2816], P(('seq', 'dp')), may hold values from -0.1875 to 0.1875
- down_weight: bfloat16 [2816, 1024], P(('seq', 'dp')), may hold values from -0.109375 to 0.109375
Outputs:
- output: bfloat16 [12, 1024, 1024], P('dp', 'seq')
- tokens_grad: float32 [12, 1024, 1024], P('dp', 'seq')
- first_values_grad: float32 [12, 1024, 1024], P('dp', 'seq')
- norm1_gain_grad: float32 [1024], P(('seq', 'dp'))
- qkv_weight_grad: float32 [1024, 3072], P(('seq', 'dp'))
- out_weight_grad: float32 [1024, 1024], P(('seq', 'dp'))
- norm2_gain_grad: float32 [1024], P(('seq', 'dp'))
- gate_weight_grad: float32 [1024, 2816], P(('seq', 'dp'))
- up_weight_grad: float32 [1024, 2816], P(('seq', 'dp'))
- down_weight_grad: float32 [2816, 1024], P(('seq', 'dp'))
Inputs may be any that keep to these rules, and one draw needn't show every extreme that they name: `lengths`: real tokens of a slot; within each index of dp one of its 3 slots, drawn from the seed, is full.
All inputs are finite; a program needn't handle non-finite values.
Results may differ from a plain program's by a relative error of at most 0.025.
Values may be sent and summed in bfloat16 or wider, within the bound.
No kernel may reach another device: no remote copies, remote signals or barrier semaphores. Data moves between devices by JAX's collectives and lax.ppermute only.
A program may use at most 320 MiB of HBM per device.

v0:
```python
import jax
import jax.numpy as jnp
from jax import lax
from jax.sharding import PartitionSpec as P

HEADS = 16
HEAD_DIM = 64


EPSILON = 1e-06


def rotate_half(values):
    half_dim = values.shape[-1] // 2
    return jnp.concatenate([-values[..., half_dim:], values[..., :half_dim]], -1)


def rotate(values, cosine, sine_table):
    return values * cosine[:, None, :] + rotate_half(values) * sine_table[:, None, :]


def rotate_back(grads, cosine, sine_table):
    return grads * cosine[:, None, :] - rotate_half(grads * sine_table[:, None, :])


def layer(whole, token_rows, value_rows, grad_rows, length, positions, cosine, sine_table):
    gain1, wqkv, wout, gain2, wgate, wup, wdown = whole
    gain1f = gain1.astype(jnp.float32)
    gain2f = gain2.astype(jnp.float32)
    rows, width = token_rows.shape
    scaling = float(HEAD_DIM) ** (-0.5)
    inputs = token_rows.astype(jnp.float32)
    inv1 = lax.rsqrt(jnp.mean(inputs * inputs, -1, keepdims=True) + EPSILON)
    normed = (inputs * inv1 * gain1f).astype(jnp.bfloat16)
    projected = jnp.dot(normed, wqkv, preferred_element_type=jnp.float32)
    queries = projected[:, :width].reshape(rows, HEADS, HEAD_DIM)
    keys_raw = projected[:, width : 2 * width].reshape(rows, HEADS, HEAD_DIM)
    values_raw = projected[:, 2 * width :].reshape(rows, HEADS, HEAD_DIM)
    query_rot = rotate(queries, cosine, sine_table).astype(jnp.bfloat16)
    key_rot = rotate(keys_raw, cosine, sine_table).astype(jnp.bfloat16)
    mixed = (
        0.5 * values_raw + 0.5 * value_rows.astype(jnp.float32).reshape(rows, HEADS, HEAD_DIM)
    ).astype(jnp.bfloat16)

    def allowed_mask(count):
        key_pos = jnp.arange(count, dtype=jnp.int32)
        return ((key_pos[None, :] <= positions[:, None]) & (key_pos[None, :] < length))[None]

    top = jnp.full((HEADS, rows), -1e30, jnp.float32)
    block_keys = lax.all_gather(key_rot, "seq", axis=0, tiled=True)
    block_values = lax.all_gather(mixed, "seq", axis=0, tiled=True)
    allowed = allowed_mask(block_keys.shape[0])
    scores = (
        jnp.einsum("chd,nhd->hcn", query_rot, block_keys, preferred_element_type=jnp.float32)
        * scaling
    )
    scores = jnp.where(allowed, scores, -1e30)
    new_top = jnp.maximum(top, jnp.max(scores, -1))
    weights = jnp.where(allowed, jnp.exp(scores - new_top[..., None]), 0.0)
    total = jnp.sum(weights, -1)
    summed = jnp.einsum(
        "hcn,nhd->hcd",
        weights.astype(jnp.bfloat16),
        block_values,
        preferred_element_type=jnp.float32,
    )
    top, total, summed = (new_top, total, summed)
    log_total = top + jnp.log(total)
    attended = jnp.transpose(summed / total[..., None], (1, 0, 2))
    attended_low = attended.reshape(rows, width).astype(jnp.bfloat16)
    middle = inputs + jnp.dot(attended_low, wout, preferred_element_type=jnp.float32)
    inv2 = lax.rsqrt(jnp.mean(middle * middle, -1, keepdims=True) + EPSILON)
    normed2 = (middle * inv2 * gain2f).astype(jnp.bfloat16)
    gate = jnp.dot(normed2, wgate, preferred_element_type=jnp.float32)
    upward = jnp.dot(normed2, wup, preferred_element_type=jnp.float32)
    sigma = jax.nn.sigmoid(gate)
    hidden = (gate * sigma * upward).astype(jnp.bfloat16)
    result = middle + jnp.dot(hidden, wdown, preferred_element_type=jnp.float32)
    grad_float = grad_rows.astype(jnp.float32)
    d_wdown = jnp.einsum("nf,nd->fd", hidden, grad_rows, preferred_element_type=jnp.float32)
    d_hidden = jnp.einsum("nd,fd->nf", grad_rows, wdown, preferred_element_type=jnp.float32)
    d_gate = (d_hidden * upward * sigma * (1.0 + gate * (1.0 - sigma))).astype(jnp.bfloat16)
    d_upward = (d_hidden * gate * sigma).astype(jnp.bfloat16)
    d_wgate = jnp.einsum("nd,nf->df", normed2, d_gate, preferred_element_type=jnp.float32)
    d_wup = jnp.einsum("nd,nf->df", normed2, d_upward, preferred_element_type=jnp.float32)
    d_normed2 = jnp.einsum(
        "nf,df->nd", d_gate, wgate, preferred_element_type=jnp.float32
    ) + jnp.einsum("nf,df->nd", d_upward, wup, preferred_element_type=jnp.float32)
    scaled2 = d_normed2 * gain2f
    d_gain2 = jnp.sum(d_normed2 * middle * inv2, 0)
    d_middle = (
        grad_float
        + inv2 * scaled2
        - middle * inv2**3 * jnp.mean(scaled2 * middle, -1, keepdims=True)
    )
    d_branch = d_middle.astype(jnp.bfloat16)
    d_wout = jnp.einsum("nc,nd->cd", attended_low, d_branch, preferred_element_type=jnp.float32)
    d_attended = (
        jnp.einsum("nd,cd->nc", d_branch, wout, preferred_element_type=jnp.float32)
        .astype(jnp.bfloat16)
        .reshape(rows, HEADS, HEAD_DIM)
    )
    delta = jnp.transpose(jnp.sum(d_attended.astype(jnp.float32) * attended, -1), (1, 0))
    block_keys = lax.all_gather(key_rot, "seq", axis=0, tiled=True)
    block_values = lax.all_gather(mixed, "seq", axis=0, tiled=True)
    count = block_keys.shape[0]
    allowed = allowed_mask(count)
    scores = (
        jnp.einsum("chd,nhd->hcn", query_rot, block_keys, preferred_element_type=jnp.float32)
        * scaling
    )
    scores = jnp.where(allowed, scores, -1e30)
    weights = jnp.where(allowed, jnp.exp(scores - log_total[..., None]), 0.0)
    d_values_piece = jnp.einsum(
        "hcn,chd->nhd", weights.astype(jnp.bfloat16), d_attended, preferred_element_type=jnp.float32
    )
    d_weights = jnp.einsum(
        "chd,nhd->hcn", d_attended, block_values, preferred_element_type=jnp.float32
    )
    d_scores = (weights * (d_weights - delta[..., None])).astype(jnp.bfloat16)
    d_query = (
        jnp.einsum("hcn,nhd->chd", d_scores, block_keys, preferred_element_type=jnp.float32)
        * scaling
    )
    d_keys_piece = (
        jnp.einsum("hcn,chd->nhd", d_scores, query_rot, preferred_element_type=jnp.float32)
        * scaling
    )
    d_keys_full = d_keys_piece
    d_values_full = d_values_piece
    d_query, d_keys_full, d_values_full = (d_query, d_keys_full, d_values_full)
    d_keys_own, d_values_own = (
        lax.psum_scatter(
            d_keys_full.astype(jnp.bfloat16), "seq", scatter_dimension=0, tiled=True
        ).astype(jnp.float32),
        lax.psum_scatter(
            d_values_full.astype(jnp.bfloat16), "seq", scatter_dimension=0, tiled=True
        ).astype(jnp.float32),
    )
    d_first = 0.5 * d_values_own.reshape(rows, width)
    d_projected = jnp.concatenate(
        [
            rotate_back(d_query, cosine, sine_table).reshape(rows, width),
            rotate_back(d_keys_own, cosine, sine_table).reshape(rows, width),
            d_first,
        ],
        -1,
    ).astype(jnp.bfloat16)
    d_wqkv = jnp.einsum("nd,ne->de", normed, d_projected, preferred_element_type=jnp.float32)
    d_normed = jnp.einsum("ne,de->nd", d_projected, wqkv, preferred_element_type=jnp.float32)
    scaled1 = d_normed * gain1f
    d_gain1 = jnp.sum(d_normed * inputs * inv1, 0)
    d_inputs = (
        d_middle + inv1 * scaled1 - inputs * inv1**3 * jnp.mean(scaled1 * inputs, -1, keepdims=True)
    )
    return (
        result.astype(jnp.bfloat16),
        d_inputs,
        d_first,
        (d_gain1, d_wqkv, d_wout, d_gain2, d_wgate, d_wup, d_wdown),
    )


def local(
    tokens,
    first_values,
    out_grad,
    lengths,
    norm1_gain,
    qkv_weight,
    out_weight,
    norm2_gain,
    gate_weight,
    up_weight,
    down_weight,
):
    micro, group_rows, width = tokens.shape
    devices = lax.axis_size("seq") * lax.axis_size("dp")
    positions = lax.axis_index("seq") * group_rows + jnp.arange(group_rows, dtype=jnp.int32)
    inverse = 10000.0 ** (-jnp.arange(0, HEAD_DIM, 2, dtype=jnp.float32) / HEAD_DIM)
    angles = positions.astype(jnp.float32)[:, None] * inverse[None, :]
    angles = jnp.concatenate([angles, angles], -1)
    cosine, sine_table = (jnp.cos(angles), jnp.sin(angles))
    shards = (norm1_gain, qkv_weight, out_weight, norm2_gain, gate_weight, up_weight, down_weight)
    running = [
        jnp.zeros((item.shape[0] * devices,) + item.shape[1:], jnp.float32) for item in shards
    ]
    outputs, token_grads, value_grads = ([], [], [])
    for index_micro in range(micro):
        whole = (
            lax.all_gather(norm1_gain, ("seq", "dp"), axis=0, tiled=True),
            lax.all_gather(qkv_weight, ("seq", "dp"), axis=0, tiled=True),
            lax.all_gather(out_weight, ("seq", "dp"), axis=0, tiled=True),
            lax.all_gather(norm2_gain, ("seq", "dp"), axis=0, tiled=True),
            lax.all_gather(gate_weight, ("seq", "dp"), axis=0, tiled=True),
            lax.all_gather(up_weight, ("seq", "dp"), axis=0, tiled=True),
            lax.all_gather(down_weight, ("seq", "dp"), axis=0, tiled=True),
        )
        result, d_inputs, d_first, grad_params = layer(
            whole,
            tokens[index_micro],
            first_values[index_micro],
            out_grad[index_micro],
            lengths[index_micro],
            positions,
            cosine,
            sine_table,
        )
        outputs.append(result)
        token_grads.append(d_inputs)
        value_grads.append(d_first)
        running = [first + second for first, second in zip(running, grad_params)]
    summed = (
        lax.psum_scatter(running[0], ("seq", "dp"), scatter_dimension=0, tiled=True),
        lax.psum_scatter(running[1], ("seq", "dp"), scatter_dimension=0, tiled=True),
        lax.psum_scatter(running[2], ("seq", "dp"), scatter_dimension=0, tiled=True),
        lax.psum_scatter(running[3], ("seq", "dp"), scatter_dimension=0, tiled=True),
        lax.psum_scatter(running[4], ("seq", "dp"), scatter_dimension=0, tiled=True),
        lax.psum_scatter(running[5], ("seq", "dp"), scatter_dimension=0, tiled=True),
        lax.psum_scatter(running[6], ("seq", "dp"), scatter_dimension=0, tiled=True),
    )
    return (
        jnp.stack(outputs),
        jnp.stack(token_grads),
        jnp.stack(value_grads),
        summed[0],
        summed[1],
        summed[2],
        summed[3],
        summed[4],
        summed[5],
        summed[6],
    )


def solution(mesh):
    return jax.shard_map(
        local,
        mesh=mesh,
        in_specs=(
            P("dp", "seq", None),
            P("dp", "seq", None),
            P("dp", "seq", None),
            P("dp"),
            P(("seq", "dp")),
            P(("seq", "dp"), None),
            P(("seq", "dp"), None),
            P(("seq", "dp")),
            P(("seq", "dp"), None),
            P(("seq", "dp"), None),
            P(("seq", "dp"), None),
        ),
        out_specs=(
            P("dp", "seq", None),
            P("dp", "seq", None),
            P("dp", "seq", None),
            P(("seq", "dp")),
            P(("seq", "dp"), None),
            P(("seq", "dp"), None),
            P(("seq", "dp")),
            P(("seq", "dp"), None),
            P(("seq", "dp"), None),
            P(("seq", "dp"), None),
        ),
        check_vma=False,
    )
```

profile of v0, /device:TPU:0, one launch (start us, length us, event | category | flops | bytes accessed | tf_op | source)
XLA Modules:
  0.0 1941.4 jit_solution(17148283050094773033)
XLA Ops:
  9.7 43.0 %all-reduce.5 = (bf16[1024]{0:T(1024)(128)(2,1)S(1)}, bf16[1024]{0:T(1024)(128)(2,1)S(1)}) all-reduce(bf16[1024]{0:T(1024)(128)(2,1)S(1)} %dynamic-update-slice, bf16[1024]{0:T(1024)(128)(2,1)S(1)} %dynamic-update-slice.1), channel_id=1, replica_groups=mesh['seq'=8,'dp'=4] {'seq','dp'}, use_global_device_ids=true, to_apply=%add | all-reduce | flops 2048 | bytes 8192
  56.0 27.4 %all-gather.12.cloned.1.call-done = bf16[1024,3072]{1,0:T(8,128)(2,1)} async-done(((bf16[32,3072]{1,0:T(8,128)(2,1)}), bf16[1024,3072]{1,0:T(8,128)(2,1)}) %all-gather.12.cloned.1.call-update) | async-done | bytes 6291472 | tf_op jit(solution)/shard_map/all_gather | solution.py:192
  83.4 4.0 fusion.166
  123.9 9.5 all-gather.14.cloned.1.call-done
  142.7 21.4 %all-gather.16.cloned.1.call-done = bf16[1024,16,64]{0,2,1:T(8,128)(2,1)} async-done(((bf16[128,16,64]{0,2,1:T(8,128)(2,1)}), bf16[1024,16,64]{0,2,1:T(8,128)(2,1)}) %all-gather.16.cloned.1.call-update) | async-done | bytes 2097168 | tf_op jit(solution)/shard_map/all_gather | solution.py:51
  164.1 7.1 fusion.200
  171.2 52.2 %all-gather.18.cloned.1.call-done = bf16[1024,1024]{1,0:T(8,128)(2,1)} async-done(((bf16[32,1024]{1,0:T(8,128)(2,1)}), bf16[1024,1024]{1,0:T(8,128)(2,1)}) %all-gather.18.cloned.1.call-update) | async-done | bytes 2097168 | tf_op jit(solution)/shard_map/all_gather | solution.py:193
  226.1 26.1 %all-gather.26.cloned.1.call-done = bf16[1024,16,64]{0,2,1:T(8,128)(2,1)} async-done(((bf16[128,16,64]{0,2,1:T(8,128)(2,1)}), bf16[1024,16,64]{0,2,1:T(8,128)(2,1)}) %all-gather.26.cloned.1.call-update) | async-done | bytes 2097168 | tf_op jit(solution)/shard_map/all_gather | solution.py:50
  261.4 21.4 %all-gather.28.cloned.1.call-done = bf16[1024,16,64]{0,2,1:T(8,128)(2,1)} async-done(((bf16[128,16,64]{0,2,1:T(8,128)(2,1)}), bf16[1024,16,64]{0,2,1:T(8,128)(2,1)}) %all-gather.28.cloned.1.call-update) | async-done | bytes 2097168 | tf_op jit(solution)/shard_map/all_gather | solution.py:51
  282.7 7.3 fusion.201
  292.6 20.3 %all-gather.30.cloned.1.call-done = bf16[1024,16,64]{0,2,1:T(8,128)(2,1)} async-done(((bf16[128,16,64]{0,2,1:T(8,128)(2,1)}), bf16[1024,16,64]{0,2,1:T(8,128)(2,1)}) %all-gather.30.cloned.1.call-update) | async-done | bytes 2097168 | tf_op jit(solution)/shard_map/all_gather | solution.py:50
  322.7 20.8 %all-gather.32.cloned.1.call-done = bf16[1024,16,64]{0,2,1:T(8,128)(2,1)} async-done(((bf16[128,16,64]{0,2,1:T(8,128)(2,1)}), bf16[1024,16,64]{0,2,1:T(8,128)(2,1)}) %all-gather.32.cloned.1.call-update) | async-done | bytes 2097168 | tf_op jit(solution)/shard_map/all_gather | solution.py:51
  343.6 7.1 fusion.199
  354.6 59.2 %all-gather.20.cloned.1.call-done = bf16[1024,2816]{1,0:T(8,128)(2,1)} async-done(((bf16[32,2816]{1,0:T(8,128)(2,1)}), bf16[1024,2816]{1,0:T(8,128)(2,1)}) %all-gather.20.cloned.1.call-update) | async-done | bytes 5767184 | tf_op jit(solution)/shard_map/all_gather | solution.py:195
  413.8 4.8 fusion.202
  418.5 64.2 %all-gather.22.cloned.1.call-done = bf16[1024,2816]{1,0:T(8,128)(2,1)} async-done(((bf16[32,2816]{1,0:T(8,128)(2,1)}), bf16[1024,2816]{1,0:T(8,128)(2,1)}) %all-gather.22.cloned.1.call-update) | async-done | bytes 5767184 | tf_op jit(solution)/shard_map/all_gather | solution.py:196
  482.8 4.8 fusion.203
  487.5 64.4 %all-gather.24.cloned.1.call-done = bf16[2816,1024]{1,0:T(8,128)(2,1)} async-done(((bf16[88,1024]{1,0:T(8,128)(2,1)}), bf16[2816,1024]{1,0:T(8,128)(2,1)}) %all-gather.24.cloned.1.call-update) | async-done | bytes 5767184 | tf_op jit(solution)/shard_map/all_gather | solution.py:197
  551.9 6.7 multiply_convert_fusion.10
  558.7 5.1 fusion.208
  592.1 7.3 fusion.42
  604.6 6.3 multiply_convert_fusion.2
  624.3 7.6 multiply_convert_fusion.1
  646.4 6.1 multiply_convert_fusion
  658.2 6.2 fusion.45
  667.0 7.7 fusion.48
  674.7 4.0 copy.101
  680.2 4.1 add_add_fusion.4
  698.5 34.5 %reduce-scatter.38.cloned.1.call-done = bf16[128,1024]{1,0:T(8,128)(2,1)} async-done(((bf16[1024,1024]{1,0:T(8,128)(2,1)}), bf16[128,1024]{1,0:T(8,128)(2,1)}) %reduce-scatter.38.cloned.1.call-update) | async-done | bytes 262160
  734.1 43.6 %reduce-scatter.42.cloned.1.call-done = bf16[128,1024]{1,0:T(8,128)(2,1)} async-done(((bf16[1024,1024]{1,0:T(8,128)(2,1)}), bf16[128,1024]{1,0:T(8,128)(2,1)}) %reduce-scatter.42.cloned.1.call-update) | async-done | bytes 262160
  778.9 43.3 %reduce-scatter.40.cloned.1.call-done = bf16[128,1024]{1,0:T(8,128)(2,1)} async-done(((bf16[1024,1024]{1,0:T(8,128)(2,1)}), bf16[128,1024]{1,0:T(8,128)(2,1)}) %reduce-scatter.40.cloned.1.call-update) | async-done | bytes 262160
  823.9 42.9 %reduce-scatter.44.cloned.1.call-done = bf16[128,1024]{1,0:T(8,128)(2,1)} async-done(((bf16[1024,1024]{1,0:T(8,128)(2,1)}), bf16[128,1024]{1,0:T(8,128)(2,1)}) %reduce-scatter.44.cloned.1.call-update) | async-done | bytes 262160
  875.1 6.5 fusion.127
  881.6 10.4 add_add_fusion
  895.0 6.0 fusion.212
  901.0 10.6 add_add_fusion.3
  914.4 6.0 fusion.214
  920.4 10.6 add_add_fusion.2
  935.0 5.9 fusion.134
  940.9 10.5 add_add_fusion.1
  951.4 4.0 fusion.63
  955.5 4.0 fusion.64
  966.6 5.4 fusion.130
  978.0 40.1 %all-reduce.4 = (f32[1024]{0:T(1024)S(1)}, f32[1024]{0:T(1024)S(1)}) all-reduce(f32[1024]{0:T(1024)S(1)} %add_add_fusion.6, f32[1024]{0:T(1024)S(1)} %add_add_fusion.5), channel_id=8, replica_groups=mesh['seq'=8,'dp'=4] {'seq','dp'}, use_global_device_ids=true, to_apply=%region_30.31.clone | all-reduce | flops 2048 | bytes 16384
  1023.9 154.6 %reduce-scatter.24.cloned.1.call-done = f32[32,3072]{1,0:T(8,128)} async-done(((f32[1024,3072]{1,0:T(8,128)}), f32[32,3072]{1,0:T(8,128)}) %reduce-scatter.24.cloned.1.call-update) | async-done | bytes 393232 | tf_op jit(solution)/shard_map/reduce_scatter | solution.py:215
  1178.5 252.9 %reduce-scatter.28.cloned.1.call-done = f32[32,2816]{1,0:T(8,128)} async-done(((f32[1024,2816]{1,0:T(8,128)}), f32[32,2816]{1,0:T(8,128)}) %reduce-scatter.28.cloned.1.call-update) | async-done | bytes 360464 | tf_op jit(solution)/shard_map/reduce_scatter | solution.py:218
  1431.4 251.5 %reduce-scatter.30.cloned.1.call-done = f32[32,2816]{1,0:T(8,128)} async-done(((f32[1024,2816]{1,0:T(8,128)}), f32[32,2816]{1,0:T(8,128)}) %reduce-scatter.30.cloned.1.call-update) | async-done | bytes 360464 | tf_op jit(solution)/shard_map/reduce_scatter | solution.py:219
  1682.9 251.4 %reduce-scatter.32.cloned.1.call-done = f32[88,1024]{1,0:T(8,128)} async-done(((f32[2816,1024]{1,0:T(8,128)}), f32[88,1024]{1,0:T(8,128)}) %reduce-scatter.32.cloned.1.call-update) | async-done | bytes 360464 | tf_op jit(solution)/shard_map/reduce_scatter | solution.py:220
  (458 shorter events, 204.1 us)
Async XLA Ops:
  7.2 76.2 %all-gather.12.cloned.1.call-start = ((), (), s32[]{:S(2)}) async-start(), calls=%async_computation.11 | async-start | bytes 6488064 | tf_op jit(solution)/shard_map/all_gather | solution.py:192
  7.9 125.5 %all-gather.14.cloned.1.call-start = ((), (), s32[]{:S(2)}) async-start(), calls=%async_computation.12 | async-start | bytes 2359296 | tf_op jit(solution)/shard_map/all_gather | solution.py:50
  52.7 43.7 %copy-start.50 = (f32[1024]{0:T(1024)}, f32[1024]{0:T(1024)S(1)}, u32[]{:S(2)}) copy-start(f32[1024]{0:T(1024)S(1)} %convert_element_type.277) | copy-start | bytes 12292
  53.5 50.1 %copy-start.85 = (f32[128,64]{0,1:T(8,128)}, f32[128,64]{0,1:T(8,128)S(1)}, u32[]{:S(2)}) copy-start(f32[128,64]{0,1:T(8,128)S(1)} %get-tuple-element.110) | copy-start | bytes 98308
  53.5 50.1 %copy-start.87 = (f32[128,64]{0,1:T(8,128)}, f32[128,64]{0,1:T(8,128)S(1)}, u32[]{:S(2)}) copy-start(f32[128,64]{0,1:T(8,128)S(1)} %get-tuple-element.109) | copy-start | bytes 98308
  55.3 32.0 %copy-start.106 = (f32[128]{0:T(128)}, f32[128]{0:T(128)S(1)}, u32[]{:S(2)}) copy-start(f32[128]{0:T(128)S(1)} %get-tuple-element.116) | copy-start | bytes 1540
  56.0 33.6 %copy-start.101 = (f32[128]{0:T(128)}, f32[128]{0:T(128)S(1)}, u32[]{:S(2)}) copy-start(f32[128]{0:T(128)S(1)} %get-tuple-element.159) | copy-start | bytes 1540
  56.0 40.4 %copy-start.108 = (f32[128]{0:T(128)}, f32[128]{0:T(128)S(1)}, u32[]{:S(2)}) copy-start(f32[128]{0:T(128)S(1)} %get-tuple-element.120) | copy-start | bytes 1540
  106.5 57.6 %all-gather.16.cloned.1.call-start = ((), (), s32[]{:S(2)}) async-start(), calls=%async_computation.13 | async-start | bytes 2359296 | tf_op jit(solution)/shard_map/all_gather | solution.py:51
  111.3 112.1 %all-gather.18.cloned.1.call-start = ((), (), s32[]{:S(2)}) async-start(), calls=%async_computation.14 | async-start | bytes 2162688 | tf_op jit(solution)/shard_map/all_gather | solution.py:193
  111.8 140.4 %all-gather.26.cloned.1.call-start = ((), (), s32[]{:S(2)}) async-start(), calls=%async_computation.18 | async-start | bytes 2359296 | tf_op jit(solution)/shard_map/all_gather | solution.py:50
  112.4 170.3 %all-gather.28.cloned.1.call-start = ((), (), s32[]{:S(2)}) async-start(), calls=%async_computation.19 | async-start | bytes 2359296 | tf_op jit(solution)/shard_map/all_gather | solution.py:51
  114.7 198.1 %all-gather.30.cloned.1.call-start = ((), (), s32[]{:S(2)}) async-start(), calls=%async_computation.20 | async-start | bytes 2359296 | tf_op jit(solution)/shard_map/all_gather | solution.py:50
  115.5 228.1 %all-gather.32.cloned.1.call-start = ((), (), s32[]{:S(2)}) async-start(), calls=%async_computation.21 | async-start | bytes 2359296 | tf_op jit(solution)/shard_map/all_gather | solution.py:51
  117.8 296.0 %all-gather.20.cloned.1.call-start = ((), (), s32[]{:S(2)}) async-start(), calls=%async_computation.15 | async-start | bytes 5947392 | tf_op jit(solution)/shard_map/all_gather | solution.py:195
  118.5 364.2 %all-gather.22.cloned.1.call-start = ((), (), s32[]{:S(2)}) async-start(), calls=%async_computation.16 | async-start | bytes 5947392 | tf_op jit(solution)/shard_map/all_gather | solution.py:196
  119.1 432.8 %all-gather.24.cloned.1.call-start = ((), (), s32[]{:S(2)}) async-start(), calls=%async_computation.17 | async-start | bytes 5947392 | tf_op jit(solution)/shard_map/all_gather | solution.py:197
  119.9 575.6 %reduce-scatter.36.cloned.1.call-start = ((), (), s32[]{:S(2)}) async-start(), calls=%async_computation.28 | async-start | bytes 2359296
  122.8 41.3 %copy-start.60 = (pred[128,1024]{1,0:T(8,128)(4,1)}, pred[128,1024]{1,0:T(8,128)(4,1)S(1)}, u32[]{:S(2)}) copy-start(pred[128,1024]{1,0:T(8,128)(4,1)S(1)} %get-tuple-element.127) | copy-start | bytes 393220
  122.8 132.7 %copy-start.59 = (pred[128,1024]{1,0:T(8,128)(4,1)}, pred[128,1024]{1,0:T(8,128)(4,1)S(1)}, u32[]{:S(2)}) copy-start(pred[128,1024]{1,0:T(8,128)(4,1)S(1)} %get-tuple-element.128) | copy-start | bytes 393220
  136.6 34.6 %copy-start.94 = (f32[16,128]{1,0:T(8,128)}, f32[16,128]{1,0:T(8,128)S(1)}, u32[]{:S(2)}) copy-start(f32[16,128]{1,0:T(8,128)S(1)} %get-tuple-element.137) | copy-start | bytes 24580
  142.7 28.5 %copy-start.97 = (f32[16,128]{1,0:T(8,128)}, f32[16,128]{1,0:T(8,128)S(1)}, u32[]{:S(2)}) copy-start(f32[16,128]{1,0:T(8,128)S(1)} %fusion) | copy-start | bytes 24580
  164.1 88.1 %copy-start.46 = (bf16[128,16,64]{0,2,1:T(8,128)(2,1)S(1)}, bf16[128,16,64]{0,2,1:T(8,128)(2,1)}, u32[]{:S(2)}) copy-start(bf16[128,16,64]{0,2,1:T(8,128)(2,1)} %get-tuple-element.91) | copy-start | bytes 786436
  171.2 84.2 %copy-start.77 = (bf16[128,16,64]{0,2,1:T(8,128)(2,1)}, bf16[128,16,64]{0,2,1:T(8,128)(2,1)S(1)}, u32[]{:S(2)}) copy-start(bf16[128,16,64]{0,2,1:T(8,128)(2,1)S(1)} %get-tuple-element.139) | copy-start | bytes 786436
  225.5 361.7 %copy-start.10 = (f32[128,1024]{1,0:T(8,128)}, f32[128,1024]{1,0:T(8,128)S(1)}, u32[]{:S(2)}) copy-start(f32[128,1024]{1,0:T(8,128)S(1)} %get-tuple-element.142) | copy-start | bytes 1572868
  255.4 27.3 %copy-start.93 = (f32[16,128]{1,0:T(8,128)}, f32[16,128]{1,0:T(8,128)S(1)}, u32[]{:S(2)}) copy-start(f32[16,128]{1,0:T(8,128)S(1)} %get-tuple-element.143) | copy-start | bytes 24580
  255.4 27.3 %copy-start.99 = (f32[16,128]{1,0:T(8,128)}, f32[16,128]{1,0:T(8,128)S(1)}, u32[]{:S(2)}) copy-start(f32[16,128]{1,0:T(8,128)S(1)} %broadcast_maximum_fusion.1) | copy-start | bytes 24580
  261.4 28.7 %copy-start.96 = (f32[16,128]{1,0:T(8,128)}, f32[16,128]{1,0:T(8,128)S(1)}, u32[]{:S(2)}) copy-start(f32[16,128]{1,0:T(8,128)S(1)} %fusion.2) | copy-start | bytes 24580
  603.4 93.9 %reduce-scatter.34.cloned.1.call-start = ((), (), s32[]{:S(2)}) async-start(), calls=%async_computation.27 | async-start | bytes 2359296
  619.0 114.0 %reduce-scatter.38.cloned.1.call-start = ((), (), s32[]{:S(2)}) async-start(), calls=%async_computation.29 | async-start | bytes 2359296
  640.1 137.7 %reduce-scatter.42.cloned.1.call-start = ((), (), s32[]{:S(2)}) async-start(), calls=%async_computation.31 | async-start | bytes 2359296
  657.9 164.3 %reduce-scatter.40.cloned.1.call-start = ((), (), s32[]{:S(2)}) async-start(), calls=%async_computation.30 | async-start | bytes 2359296
  666.9 200.0 %reduce-scatter.44.cloned.1.call-start = ((), (), s32[]{:S(2)}) async-start(), calls=%async_computation.32 | async-start | bytes 2359296
  678.8 345.2 %reduce-scatter.26.cloned.1.call-start = ((), (), s32[]{:S(2)}) async-start(), calls=%async_computation.23 | async-start | bytes 4325376 | tf_op jit(solution)/shard_map/reduce_scatter | solution.py:216
  684.4 494.2 %reduce-scatter.24.cloned.1.call-start = ((), (), s32[]{:S(2)}) async-start(), calls=%async_computation.22 | async-start | bytes 12976128 | tf_op jit(solution)/shard_map/reduce_scatter | solution.py:215
  694.2 174.5 %copy-start.88 = (f32[128,64]{0,1:T(8,128)S(1)}, f32[128,64]{0,1:T(8,128)}, u32[]{:S(2)}) copy-start(f32[128,64]{0,1:T(8,128)} %copy-done.87) | copy-start | bytes 98308
  695.5 186.2 %copy-start.66 = (bf16[128,16,64]{0,2,1:T(8,128)(2,1)}, bf16[128,16,64]{0,2,1:T(8,128)(2,1)S(1)}, u32[]{:S(2)}) copy-start(bf16[128,16,64]{0,2,1:T(8,128)(2,1)S(1)} %get-tuple-element.97) | copy-start | bytes 786436
  697.3 175.4 %copy-start.86 = (f32[128,64]{0,1:T(8,128)S(1)}, f32[128,64]{0,1:T(8,128)}, u32[]{:S(2)}) copy-start(f32[128,64]{0,1:T(8,128)} %copy-done.85) | copy-start | bytes 98308
  892.1 539.3 %reduce-scatter.28.cloned.1.call-start = ((), (), s32[]{:S(2)}) async-start(), calls=%async_computation.24 | async-start | bytes 11894784 | tf_op jit(solution)/shard_map/reduce_scatter | solution.py:218
  911.6 771.2 %reduce-scatter.30.cloned.1.call-start = ((), (), s32[]{:S(2)}) async-start(), calls=%async_computation.25 | async-start | bytes 11894784 | tf_op jit(solution)/shard_map/reduce_scatter | solution.py:219
  931.1 1003.2 %reduce-scatter.32.cloned.1.call-start = ((), (), s32[]{:S(2)}) async-start(), calls=%async_computation.26 | async-start | bytes 11894784 | tf_op jit(solution)/shard_map/reduce_scatter | solution.py:220
  974.4 44.9 %copy-start.25 = (f32[128,1024]{1,0:T(8,128)S(1)}, f32[128,1024]{1,0:T(8,128)}, u32[]{:S(2)}) copy-start(f32[128,1024]{1,0:T(8,128)} %copy-done.23) | copy-start | bytes 1572868
  974.4 44.9 %copy-start.119 = (f32[128]{0:T(128)S(1)}, f32[128]{0:T(128)}, u32[]{:S(2)}) copy-start(f32[128]{0:T(128)} %get-tuple-element.119) | copy-start | bytes 1540
  974.4 44.9 %copy-start.120 = (f32[128]{0:T(128)S(1)}, f32[128]{0:T(128)}, u32[]{:S(2)}) copy-start(f32[128]{0:T(128)} %get-tuple-element.160) | copy-start | bytes 1540
  974.4 44.9 %copy-start.121 = (f32[128]{0:T(128)S(1)}, f32[128]{0:T(128)}, u32[]{:S(2)}) copy-start(f32[128]{0:T(128)} %get-tuple-element.115) | copy-start | bytes 1540
  977.9 44.7 %copy-start.56 = (f32[1,128,1024]{2,1,0:T(8,128)S(1)}, f32[1,128,1024]{2,1,0:T(8,128)}, u32[]{:S(2)}) copy-start(f32[1,128,1024]{2,1,0:T(8,128)} %copy.78) | copy-start | bytes 1572868
  977.9 44.7 %copy-start.57 = (f32[1,128,1024]{2,1,0:T(8,128)S(1)}, f32[1,128,1024]{2,1,0:T(8,128)}, u32[]{:S(2)}) copy-start(f32[1,128,1024]{2,1,0:T(8,128)} %copy.77) | copy-start | bytes 1572868
  977.9 44.7 %copy-start.58 = (f32[1,128,1024]{2,1,0:T(8,128)S(1)}, f32[1,128,1024]{2,1,0:T(8,128)}, u32[]{:S(2)}) copy-start(f32[1,128,1024]{2,1,0:T(8,128)} %copy.76) | copy-start | bytes 1572868
  (107 other events, 516.4 us)
Sparse Core Ops, SparseCore 0:
  10.9 72.4 all-gather.11
  106.6 26.7 all-gather.13
  135.9 28.1 all-gather.15
  166.9 56.4 all-gather.17
  225.1 27.0 all-gather.25
  254.5 28.1 all-gather.27
  284.6 28.2 all-gather.29
  315.3 28.1 all-gather.31
  346.4 67.3 all-gather.19
  416.5 66.2 all-gather.21
  485.6 66.2 all-gather.23
  603.5 40.1 reduce-scatter.35
  647.4 41.2 reduce-scatter.33
  691.8 41.1 reduce-scatter.37
  736.5 41.2 reduce-scatter.41
  780.9 41.1 reduce-scatter.39
  825.6 41.2 reduce-scatter.43
  869.6 147.9 reduce-scatter.25
  1024.2 154.2 reduce-scatter.23
  1181.4 250.0 reduce-scatter.27
  1434.4 248.4 reduce-scatter.29
  1685.9 248.4 reduce-scatter.31
where the time goes:
time: 1950 us; the launch traced here: 1940 us
  waiting for transfers between devices  1470 us (75%)
  matrix products  252 us (13%)
  blocking collectives  83.1 us (4%)
  local copies, waits for them, and re-layouts  75.2 us (4%)
  other arithmetic  46.6 us (2%)
    reduce_scatter x1, waiting for transfers between devices, local(): lax.psum_scatter(running[4], ('seq', 'dp'), scatter_dimension=0, tiled=True)  253 us
    reduce_scatter x1, waiting for transfers between devices, local(): lax.psum_scatter(running[5], ('seq', 'dp'), scatter_dimension=0, tiled=True)  251 us
    reduce_scatter x1, waiting for transfers between devices, local(): lax.psum_scatter(running[6], ('seq', 'dp'), scatter_dimension=0, tiled=True)  251 us
    unnamed x28, waiting for transfers between devices  169 us
    reduce_scatter x1, waiting for transfers between devices, local(): lax.psum_scatter(running[1], ('seq', 'dp'), scatter_dimension=0, tiled=True)  155 us
    unnamed x2, blocking collectives  83.1 us
    all_gather x1, waiting for transfers between devices, local(): lax.all_gather(down_weight, ('seq', 'dp'), axis=0, tiled=True)  64.4 us
    all_gather x1, waiting for transfers between devices, local(): lax.all_gather(up_weight, ('seq', 'dp'), axis=0, tiled=True)  64.2 us
  transfers between devices with their start and end apart: 22, of which 19 were waited for; matrix products, arithmetic and copies ran while one was open for 14% of the time, Pallas kernels for 0%

commit v1 on v0

v1 whole, which is shorter than its diff:
```python
import functools

import jax
import jax.numpy as jnp
from jax import lax
from jax.experimental import pallas as pl
from jax.experimental.pallas import tpu as pltpu
from jax.sharding import PartitionSpec as P

HEADS = 16
HEAD_DIM = 64
EPSILON = 1e-06
CORES = 2
OUTER = 2
BLOCK = 256
NEG = -1e30
F32 = jnp.float32
BF16 = jnp.bfloat16
VMEM_LIMIT = 60 * 1024 * 1024


def dot_nn(a, b):
    return lax.dot_general(a, b, (((1,), (0,)), ((), ())), preferred_element_type=F32)


def dot_nt(a, b):
    return lax.dot_general(a, b, (((1,), (1,)), ((), ())), preferred_element_type=F32)


def dot_tn(a, b):
    return lax.dot_general(a, b, (((0,), (0,)), ((), ())), preferred_element_type=F32)


def turned(u):
    half = HEAD_DIM // 2
    width = u.shape[1]
    if width % 128:
        parts = []
        for h in range(width // HEAD_DIM):
            lo = h * HEAD_DIM
            parts += [u[:, lo + half : lo + HEAD_DIM], u[:, lo : lo + half]]
        return jnp.concatenate(parts, axis=1)
    lane = lax.broadcasted_iota(jnp.int32, u.shape, 1) % HEAD_DIM
    return jnp.where(lane < half, pltpu.roll(u, width - half, 1), pltpu.roll(u, half, 1))


def head_mask(shape, h):
    lane = lax.broadcasted_iota(jnp.int32, shape, 1)
    return (lane >= h * HEAD_DIM) & (lane < (h + 1) * HEAD_DIM)


def own_head(u, h):
    if u.shape[1] == HEAD_DIM:
        return u
    return jnp.where(head_mask(u.shape, h), u, jnp.zeros_like(u))


def join_heads(parts):
    out = parts[0]
    for h in range(1, len(parts)):
        out = jnp.where(head_mask(out.shape, h), parts[h], out)
    return out


def fill_rows(seat, refs, dest, rows):
    for ref, ms in refs:
        for j, m in enumerate(ms):
            at = pl.multiple_of((seat ^ m) * rows, rows)
            dest[pl.ds(at, rows), :] = ref[j, 0]


def attn_fwd_kernel(
    order, seat_ref, len_ref, xa0, xa1, xb0, xb1, w_ref, v1_ref, cos_ref, sin_ref,
    qkv_out, ot_out, send_out, lse_out, r1_out, xbuf, vt,
):
    slot = pl.program_id(0)
    seat = seat_ref[0]
    rows = xa0.shape[2]
    length = len_ref[slot]
    total = xbuf.shape[0]
    wide = w_ref.shape[1] // 3
    heads = wide // HEAD_DIM
    blocks = total // BLOCK
    per = BLOCK // rows
    fill_rows(seat, zip((xa0, xa1, xb0, xb1), order), xbuf, rows)
    for b in range(blocks):
        at = slice(b * BLOCK, (b + 1) * BLOCK)
        x = xbuf[at, :]
        xf = x.astype(F32)
        r1 = lax.rsqrt(jnp.mean(xf * xf, axis=1, keepdims=True) + EPSILON)
        qkv = dot_nn(x, w_ref[...]) * r1
        cosine = cos_ref[at, :]
        sine = sin_ref[at, :]
        q = qkv[:, :wide]
        k = qkv[:, wide : 2 * wide]
        v = qkv[:, 2 * wide :]
        q = (q * cosine + turned(q) * sine) * (HEAD_DIM**-0.5)
        k = k * cosine + turned(k) * sine
        v1 = v1_ref[b * per : (b + 1) * per, 0].reshape(BLOCK, wide).astype(F32)
        vm = 0.5 * v + 0.5 * v1
        qkv_out[0, at, :wide] = q.astype(BF16)
        qkv_out[0, at, wide : 2 * wide] = k.astype(BF16)
        qkv_out[0, at, 2 * wide :] = vm.astype(BF16)
        vt[:, at] = vm.T.astype(BF16)
        r1_out[0, at, :] = jnp.broadcast_to(r1, (BLOCK, r1_out.shape[2]))
    for b in range(blocks):
        at = slice(b * BLOCK, (b + 1) * BLOCK)
        count = (b + 1) * BLOCK
        q = qkv_out[0, at, :wide]
        query = b * BLOCK + lax.broadcasted_iota(jnp.int32, (1, BLOCK), 1)
        last = jnp.minimum(query, length - 1)
        key = lax.broadcasted_iota(jnp.int32, (count, BLOCK), 0)
        allowed = key <= last
        ots = []
        for h in range(heads):
            k = own_head(qkv_out[0, :count, wide : 2 * wide], h)
            scores = jnp.where(allowed, dot_nt(k, q), NEG)
            top = jnp.max(scores, axis=0, keepdims=True)
            weights = jnp.exp(scores - top)
            total_w = jnp.sum(weights, axis=0, keepdims=True)
            ot = dot_nn(vt[h * HEAD_DIM : (h + 1) * HEAD_DIM, :count], weights.astype(BF16))
            ots.append(ot / total_w)
            lse_out[0, h : h + 1, at] = top + jnp.log(total_w)
        ot = jnp.concatenate(ots, axis=0)
        ot_out[0, :, at] = ot
        o = ot.T.astype(BF16)
        half = total // OUTER
        spread = send_out.shape[0] // OUTER
        group = (b * BLOCK) // half
        start = b * BLOCK - group * half
        for j in range(spread):
            send_out[group * spread + j, 0, start : start + BLOCK, :] = o


def attn_fwd(seat, lengths, xs, w, v1, cosine, sine, order):
    xa0, xa1, xb0, xb1 = xs
    spread, micro, rows, width = xa0.shape
    total = rows * 4 * spread
    wide = w.shape[1] // 3
    heads = wide // HEAD_DIM
    smem = pl.BlockSpec(memory_space=pltpu.SMEM)
    whole = lambda a: pl.BlockSpec(a.shape, lambda i: (0,) * a.ndim)
    xspec = pl.BlockSpec((spread, 1, rows, width), lambda i: (0, i, 0, 0))
    pairs = total * total // 2 * micro * wide
    return pl.pallas_call(
        functools.partial(attn_fwd_kernel, order),
        grid=(micro,),
        in_specs=[
            smem, smem, xspec, xspec, xspec, xspec, whole(w),
            pl.BlockSpec((v1.shape[0], 1, rows, wide), lambda i: (0, i, 0, 0)),
            whole(cosine), whole(sine),
        ],
        out_specs=[
            pl.BlockSpec((1, total, 3 * wide), lambda i: (i, 0, 0)),
            pl.BlockSpec((1, wide, total), lambda i: (i, 0, 0)),
            pl.BlockSpec((OUTER * spread, 1, total // OUTER, wide), lambda i: (0, i, 0, 0)),
            pl.BlockSpec((1, heads, total), lambda i: (i, 0, 0)),
            pl.BlockSpec((1, total, 128), lambda i: (i, 0, 0)),
        ],
        out_shape=[
            jax.ShapeDtypeStruct((micro, total, 3 * wide), BF16),
            jax.ShapeDtypeStruct((micro, wide, total), F32),
            jax.ShapeDtypeStruct((OUTER * spread, micro, total // OUTER, wide), BF16),
            jax.ShapeDtypeStruct((micro, heads, total), F32),
            jax.ShapeDtypeStruct((micro, total, 128), F32),
        ],
        scratch_shapes=[pltpu.VMEM((total, width), BF16), pltpu.VMEM((wide, total), BF16)],
        compiler_params=pltpu.CompilerParams(vmem_limit_bytes=VMEM_LIMIT),
        cost_estimate=pl.CostEstimate(
            flops=2 * micro * total * width * 3 * wide + 16 * pairs,
            bytes_accessed=2 * micro * total * (width + 16 * wide),
            transcendentals=micro * heads * total * total // 2,
        ),
        name="attn_fwd",
    )(seat, lengths, xa0, xa1, xb0, xb1, w, v1, cosine, sine)


def attn_bwd_kernel(
    order, seat_ref, len_ref, xa0, xa1, xb0, xb1, w_ref, do_ref, cos_ref, sin_ref, qkv_ref, ot_ref,
    lse_ref, r1_ref, dv_out, za0, za1, zb0, zb1, dw_out, xbuf, dobuf, dqt, ebuf, zbuf, dw,
):
    slot = pl.program_id(0)
    seat = seat_ref[0]
    rows = xa0.shape[2]
    length = len_ref[slot]
    total = xbuf.shape[0]
    wide = w_ref.shape[1] // 3
    heads = wide // HEAD_DIM
    blocks = total // BLOCK
    per = BLOCK // rows
    fill_rows(seat, zip((xa0, xa1, xb0, xb1), order), xbuf, rows)
    for j in range(do_ref.shape[0]):
        dobuf[j * rows : (j + 1) * rows, :] = do_ref[j, 0]
    deltas = []
    for h in range(heads):
        part = slice(h * HEAD_DIM, (h + 1) * HEAD_DIM)
        deltas.append(None)
    dot_t = dobuf[...].astype(F32).T
    for h in range(heads):
        part = slice(h * HEAD_DIM, (h + 1) * HEAD_DIM)
        deltas[h] = jnp.sum(dot_t[part, :] * ot_ref[0, part, :], axis=0, keepdims=True)
    dqt[...] = jnp.zeros_like(dqt)
    for b in range(blocks):
        at = slice(b * BLOCK, (b + 1) * BLOCK)
        later = slice(b * BLOCK, total)
        count = total - b * BLOCK
        k = qkv_ref[0, at, wide : 2 * wide]
        v = qkv_ref[0, at, 2 * wide :]
        kt = k.astype(F32).T.astype(BF16)
        q = qkv_ref[0, later, :wide]
        d_o = dobuf[later, :]
        query = b * BLOCK + lax.broadcasted_iota(jnp.int32, (1, count), 1)
        last = jnp.minimum(query, length - 1)
        key = b * BLOCK + lax.broadcasted_iota(jnp.int32, (BLOCK, count), 0)
        allowed = key <= last
        dks, dvs = [], []
        for h in range(heads):
            part = slice(h * HEAD_DIM, (h + 1) * HEAD_DIM)
            scores = jnp.where(allowed, dot_nt(own_head(k, h), q), NEG)
            weights = jnp.exp(scores - lse_ref[0, h : h + 1, later])
            d_weights = dot_nt(own_head(v, h), d_o)
            ds = (weights * (d_weights - deltas[h][:, later])).astype(BF16)
            dvs.append(dot_nn(weights.astype(BF16), d_o))
            dks.append(dot_nn(ds, q))
            dqt[part, later] += dot_nn(kt[part, :], ds)
        cosine = cos_ref[at, :]
        sine = sin_ref[at, :]
        r1 = r1_ref[0, at, 0:1]
        dk = join_heads(dks)
        dk = dk * cosine - turned(dk) * sine
        dv = 0.5 * join_heads(dvs)
        dv_out[b * per : (b + 1) * per, 0] = dv.astype(BF16).reshape(per, rows, wide)
        ebuf[at, wide : 2 * wide] = (dk * r1).astype(BF16)
        ebuf[at, 2 * wide :] = (dv * r1).astype(BF16)
    for b in range(blocks):
        at = slice(b * BLOCK, (b + 1) * BLOCK)
        dq = dqt[:, at].T * (HEAD_DIM**-0.5)
        dq = dq * cos_ref[at, :] - turned(dq) * sin_ref[at, :]
        ebuf[at, :wide] = (dq * r1_ref[0, at, 0:1]).astype(BF16)
        zbuf[at, :] = dot_nt(ebuf[at, :], w_ref[...]).astype(BF16)
    for ref, ms in zip((za0, za1, zb0, zb1), order):
        for j, m in enumerate(ms):
            ref[j, 0] = zbuf[pl.ds(pl.multiple_of((seat ^ m) * rows, rows), rows), :]
    grown = dot_tn(xbuf[...], ebuf[...])

    @pl.when(slot == 0)
    def _():
        dw[...] = grown

    @pl.when(slot > 0)
    def _():
        dw[...] += grown

    @pl.when(slot == pl.num_programs(0) - 1)
    def _():
        dw_out[...] = dw[...].astype(BF16)


def attn_bwd(seat, lengths, xs, w, d_o, cosine, sine, qkv, ot, lse, r1, order):
    xa0 = xs[0]
    spread, micro, rows, width = xa0.shape
    total = rows * 4 * spread
    wide = w.shape[1] // 3
    heads = wide // HEAD_DIM
    smem = pl.BlockSpec(memory_space=pltpu.SMEM)
    whole = lambda a: pl.BlockSpec(a.shape, lambda i: (0,) * a.ndim)
    xspec = pl.BlockSpec((spread, 1, rows, width), lambda i: (0, i, 0, 0))
    vspec = pl.BlockSpec((d_o.shape[0], 1, rows, wide), lambda i: (0, i, 0, 0))
    zshape = jax.ShapeDtypeStruct(xa0.shape, BF16)
    pairs = total * total // 2 * micro * wide
    return pl.pallas_call(
        functools.partial(attn_bwd_kernel, order),
        grid=(micro,),
        in_specs=[
            smem, smem, xspec, xspec, xspec, xspec, whole(w), vspec, whole(cosine), whole(sine),
            pl.BlockSpec((1, total, 3 * wide), lambda i: (i, 0, 0)),
            pl.BlockSpec((1, wide, total), lambda i: (i, 0, 0)),
            pl.BlockSpec((1, heads, total), lambda i: (i, 0, 0)),
            pl.BlockSpec((1, total, 128), lambda i: (i, 0, 0)),
        ],
        out_specs=[vspec, xspec, xspec, xspec, xspec, pl.BlockSpec(w.shape, lambda i: (0, 0))],
        out_shape=[
            jax.ShapeDtypeStruct(d_o.shape, BF16), zshape, zshape, zshape, zshape,
            jax.ShapeDtypeStruct(w.shape, BF16),
        ],
        scratch_shapes=[
            pltpu.VMEM((total, width), BF16),
            pltpu.VMEM((total, wide), BF16),
            pltpu.VMEM((wide, total), F32),
            pltpu.VMEM((total, 3 * wide), BF16),
            pltpu.VMEM((total, width), BF16),
            pltpu.VMEM(w.shape, F32),
        ],
        compiler_params=pltpu.CompilerParams(vmem_limit_bytes=VMEM_LIMIT),
        cost_estimate=pl.CostEstimate(
            flops=4 * micro * total * width * 3 * wide + 40 * pairs,
            bytes_accessed=2 * micro * total * (2 * width + 24 * wide),
            transcendentals=micro * heads * total * total // 2,
        ),
        name="attn_bwd",
    )(seat, lengths, *xs, w, d_o, cosine, sine, qkv, ot, lse, r1)


def ff_kernel(
    seat_ref, xa, xb, ga, gb, oa_lo, ob_lo, oa_hi, ob_hi, wout_ref, wg_ref, wu_ref, wd_ref,
    za, zb, fa, fb, y_out, o_out, dwg_out, dwu_out, dwd_out, dwg, dwu, dwd,
):
    step = pl.program_id(0)
    core = seat_ref[0] % CORES
    micro, rows, width = xa.shape[1:]
    many = micro * rows

    def attended(mine, other):
        parts = []
        for j in range(mine.shape[0]):
            a = mine[j].reshape(many, mine.shape[3])
            b = other[j].reshape(many, other.shape[3])
            parts += [jnp.where(core == 0, a, b), jnp.where(core == 0, b, a)]
        return jnp.concatenate(parts, axis=1)

    @pl.when(step == 0)
    def _():
        dwg[...] = jnp.zeros_like(dwg)
        dwu[...] = jnp.zeros_like(dwu)
        dwd[...] = jnp.zeros_like(dwd)

    for x_ref, g_ref, mine, other, z_ref, f_ref, own in (
        (xa, ga, oa_lo, ob_lo, za, fa, True),
        (xb, gb, oa_hi, ob_hi, zb, fb, False),
    ):
        o = attended(mine, other)
        x = x_ref[0].reshape(many, width).astype(F32)
        g = g_ref[0].reshape(many, width)
        y = x + dot_nn(o, wout_ref[...])
        r2 = lax.rsqrt(jnp.mean(y * y, axis=1, keepdims=True) + EPSILON)
        hn = (y * r2).astype(BF16)
        if own:

            @pl.when(step == 0)
            def _():
                y_out[...] = y
                o_out[...] = o

        gate = dot_nn(hn, wg_ref[...])
        up = dot_nn(hn, wu_ref[...])
        sigma = jax.nn.sigmoid(gate)
        act = gate * sigma
        hid = (act * up).astype(BF16)
        dhid = dot_nt(g, wd_ref[...])
        dgate = (dhid * up * sigma * (1.0 + gate * (1.0 - sigma))).astype(BF16)
        dup = (dhid * act).astype(BF16)
        f_ref[0] = dot_nn(hid, wd_ref[...]).astype(BF16)
        z_ref[0] = (dot_nt(dgate, wg_ref[...]) + dot_nt(dup, wu_ref[...])).astype(BF16)
        dwg[...] += dot_tn(hn, dgate)
        dwu[...] += dot_tn(hn, dup)
        dwd[...] += dot_tn(hid, g)

    @pl.when(step == pl.num_programs(0) - 1)
    def _():
        dwg_out[...] = dwg[...].astype(BF16)
        dwu_out[...] = dwu[...].astype(BF16)
        dwd_out[...] = dwd[...].astype(BF16)


def feed_forward(seat, xa, xb, ga, gb, oa, ob, wout, wg, wu, wd):
    spread, micro, rows, width = xa.shape
    many = micro * rows
    group = spread * CORES
    wide = oa.shape[3]
    fan = wg.shape[1]
    whole = lambda a: pl.BlockSpec(a.shape, lambda i, s: (0,) * a.ndim)
    xspec = pl.BlockSpec((1, micro, rows, width), lambda i, s: (i, 0, 0, 0))

    def ospec(low):
        return pl.BlockSpec(
            (oa.shape[0], micro, rows, wide),
            lambda i, s: (0, 0, (s[0] % group) ^ (2 * i + low), 0),
        )

    zspec = pl.BlockSpec((1, many, width), lambda i, s: (i, 0, 0))
    zshape = jax.ShapeDtypeStruct((spread, many, width), BF16)
    fixed = lambda shape: pl.BlockSpec(shape, lambda i, s: (0,) * len(shape))
    tokens = group * many
    return pl.pallas_call(
        ff_kernel,
        grid_spec=pltpu.PrefetchScalarGridSpec(
            num_scalar_prefetch=1,
            grid=(spread,),
            in_specs=[
                xspec, xspec, xspec, xspec, ospec(0), ospec(0), ospec(1), ospec(1),
                whole(wout), whole(wg), whole(wu), whole(wd),
            ],
            out_specs=[
                zspec, zspec, zspec, zspec, fixed((many, width)), fixed((many, width)),
                fixed(wg.shape), fixed(wu.shape), fixed(wd.shape),
            ],
            scratch_shapes=[
                pltpu.VMEM(wg.shape, F32), pltpu.VMEM(wu.shape, F32), pltpu.VMEM(wd.shape, F32),
            ],
        ),
        out_shape=[
            zshape, zshape, zshape, zshape,
            jax.ShapeDtypeStruct((many, width), F32),
            jax.ShapeDtypeStruct((many, width), BF16),
            jax.ShapeDtypeStruct(wg.shape, BF16),
            jax.ShapeDtypeStruct(wu.shape, BF16),
            jax.ShapeDtypeStruct(wd.shape, BF16),
        ],
        compiler_params=pltpu.CompilerParams(vmem_limit_bytes=VMEM_LIMIT),
        cost_estimate=pl.CostEstimate(
            flops=2 * tokens * width * (width + 9 * fan),
            bytes_accessed=2 * tokens * width * 6 + 20 * width * fan,
            transcendentals=tokens * fan,
        ),
        name="feed_forward",
    )(seat, xa, xb, ga, gb, oa, ob, oa, ob, wout, wg, wu, wd)


def rope_tables(total, wide):
    positions = jnp.arange(total, dtype=jnp.int32).astype(F32)
    inverse = 10000.0 ** (-jnp.arange(0, HEAD_DIM, 2, dtype=F32) / HEAD_DIM)
    angles = positions[:, None] * inverse[None, :]
    cosine, sine = jnp.cos(angles), jnp.sin(angles)
    cosine = jnp.tile(cosine, (1, 2 * wide // HEAD_DIM))
    sine = jnp.tile(jnp.concatenate([-sine, sine], -1), (1, wide // HEAD_DIM))
    return cosine, sine


def local(
    tokens, first_values, out_grad, lengths, norm1_gain, qkv_weight, out_weight, norm2_gain,
    gate_weight, up_weight, down_weight,
):
    micro, rows, width = tokens.shape
    seats, depth = lax.axis_size("seq"), lax.axis_size("dp")
    devices = seats * depth
    seat = lax.axis_index("seq")
    group = seats // OUTER
    spread = group // CORES
    outer = seat // group
    total = seats * rows
    wide = width // seats
    held = qkv_weight.shape[0]
    fan_rows = down_weight.shape[0]
    fan = fan_rows * devices
    piece = fan // seats
    slab = OUTER * piece
    padded = -(-slab // 128) * 128
    many = micro * rows
    seat_arr = jnp.reshape(seat, (1,)).astype(jnp.int32)

    def swap(value, mask):
        return lax.ppermute(value, "seq", [(i, i ^ mask) for i in range(seats)])

    same_core = [[i for i in range(seats) if i % CORES == c] for c in range(CORES)]
    same_outer = [list(range(o * group, (o + 1) * group)) for o in range(OUTER)]
    every = ("seq", "dp")

    gain1 = norm1_gain.astype(F32)[:, None]
    gain2 = norm2_gain.astype(F32)[:, None]

    inner = [2 * j for j in range(spread)]
    across = [group + 2 * j for j in range(spread)]
    xa0 = jnp.stack([tokens] + [swap(tokens, m) for m in inner[1:]])
    xb0 = swap(xa0, 1)
    xa1 = jnp.stack([swap(tokens, m) for m in across])
    xb1 = swap(xa1, 1)
    order = (
        tuple(inner), tuple(across), tuple(m + 1 for m in inner), tuple(m + 1 for m in across),
    )
    xs = (xa0, xa1, xb0, xb1)

    wqkv = (qkv_weight.astype(F32) * gain1).astype(BF16)
    wqkv = wqkv.reshape(held, 3, seats, wide).transpose(2, 0, 1, 3).reshape(seats, 1, held, 3 * wide)
    wqkv = jnp.broadcast_to(wqkv, (seats, depth, held, 3 * wide)).reshape(devices, held, 3 * wide)
    wqkv = lax.all_to_all(wqkv, every, split_axis=0, concat_axis=0, tiled=True)
    wqkv = wqkv.reshape(width, 3 * wide)

    v1 = first_values.reshape(micro, rows, seats, wide).transpose(2, 0, 1, 3)
    v1 = lax.all_to_all(v1, "seq", split_axis=0, concat_axis=0, tiled=True)

    def columns(weight):
        scaled = (weight.astype(F32) * gain2).astype(BF16)
        return scaled.reshape(held, OUTER, group, piece).transpose(2, 0, 1, 3).reshape(group, held, slab)

    pair = jnp.concatenate([columns(gate_weight), columns(up_weight)], -1)
    pair = lax.all_to_all(
        pair, "seq", split_axis=0, concat_axis=0, tiled=True, axis_index_groups=same_outer
    )

    def both_outer(value):
        other = swap(value, group)
        return jnp.where(outer == 0, jnp.stack([value, other]), jnp.stack([other, value]))

    pair = lax.all_gather(both_outer(pair), "dp", axis=0)
    pair = pair.transpose(1, 2, 0, 3, 4).reshape(width, 2 * slab)
    grow = ((0, 0), (0, padded - slab))
    wg = jnp.pad(pair[:, :slab], grow)
    wu = jnp.pad(pair[:, slab:], grow)

    tail = jnp.concatenate([down_weight, out_weight], 0)
    tail = lax.all_gather(both_outer(tail), "dp", axis=0)
    wd = tail[:, :, :fan_rows].transpose(1, 0, 2, 3).reshape(slab, width)
    wd = jnp.pad(wd, ((0, padded - slab), (0, 0)))
    wout = tail[:, :, fan_rows:].transpose(1, 0, 2, 3)[:, None, None]
    inner_at = (seat % group) // CORES
    core = seat % CORES
    pieces = jnp.stack([wout] + [swap(wout, m) for m in inner[1:]])
    wout = jnp.concatenate([pieces[inner_at ^ j] for j in range(spread)], 1)
    other = swap(wout, 1)
    wout = jnp.where(
        core == 0, jnp.concatenate([wout, other], 2), jnp.concatenate([other, wout], 2)
    ).reshape(width, width)

    ga = jnp.stack([out_grad] + [swap(out_grad, m) for m in inner[1:]])
    gb = swap(ga, 1)

    cosine, sine = rope_tables(total, wide)
    qkv, ot, send, lse, r1 = attn_fwd(seat_arr, lengths, xs, wqkv, v1, cosine, sine, order)
    oa = lax.all_to_all(
        send, "seq", split_axis=0, concat_axis=0, tiled=True, axis_index_groups=same_core
    )
    ob = swap(oa, 1)
    za, zb, fa, fb, y, o_own, dwg, dwu, dwd = feed_forward(
        seat_arr, xa0, xb0, ga, gb, oa, ob, wout, wg, wu, wd
    )

    def gathered(mine, theirs):
        joined = (mine.astype(F32) + swap(theirs, 1).astype(F32)).astype(BF16)
        out = joined[0].astype(F32)
        for j in range(1, spread):
            out = out + swap(joined[j], inner[j]).astype(F32)
        return out

    z = gathered(za, zb)
    grad = out_grad.reshape(many, width).astype(F32)
    r2 = lax.rsqrt(jnp.mean(y * y, -1, keepdims=True) + EPSILON)
    dy = grad + r2 * z - y * (r2 * r2 * r2) * jnp.mean(z * y, -1, keepdims=True)
    dyb = dy.astype(BF16)
    d_o = dot_nt(dyb, wout).astype(BF16)
    d_o = d_o.reshape(micro, rows, seats, wide).transpose(2, 0, 1, 3)
    d_o = lax.all_to_all(d_o, "seq", split_axis=0, concat_axis=0, tiled=True)
    output = (y + gathered(fa, fb)).astype(BF16).reshape(tokens.shape)

    pair = jnp.concatenate([dwg[:, :slab], dwu[:, :slab]], -1)
    pair = pair.reshape(OUTER, group, depth, held, 2 * slab).transpose(2, 0, 1, 3, 4)
    dwd = dwd[:slab].reshape(OUTER, depth, fan_rows, width).transpose(1, 0, 2, 3)
    dwd = lax.psum_scatter(dwd, "dp", scatter_dimension=0)
    pair = lax.psum_scatter(pair, "dp", scatter_dimension=0)

    def own_outer(value):
        mine = jnp.where(outer == 0, value[0], value[1])
        theirs = jnp.where(outer == 0, value[1], value[0])
        return mine.astype(F32) + swap(theirs, group).astype(F32)

    down_grad = own_outer(dwd)
    pair = own_outer(pair).astype(BF16)
    pair = lax.all_to_all(
        pair, "seq", split_axis=0, concat_axis=0, tiled=True, axis_index_groups=same_outer
    )
    pair = pair.reshape(group, held, 2, OUTER, piece).transpose(2, 1, 3, 0, 4).reshape(2, held, fan)
    pair = pair.astype(F32)
    gate_grad, up_grad = pair[0] * gain2, pair[1] * gain2
    gain2_grad = jnp.sum(
        pair[0] * gate_weight.astype(F32) + pair[1] * up_weight.astype(F32), -1
    )

    d_wout = dot_tn(o_own, dyb).astype(BF16)
    out_grad_w = lax.psum_scatter(
        d_wout.reshape(devices, held, width), every, scatter_dimension=0
    ).astype(F32)

    dv, xz0, xz1, xw0, xw1, dwq = attn_bwd(
        seat_arr, lengths, xs, wqkv, d_o, cosine, sine, qkv, ot, lse, r1, order
    )
    dv = lax.all_to_all(dv, "seq", split_axis=0, concat_axis=0, tiled=True)
    d_first = dv.transpose(1, 2, 0, 3).reshape(tokens.shape).astype(F32)
    dwq = lax.all_to_all(
        dwq.reshape(devices, held, 3 * wide), every, split_axis=0, concat_axis=0, tiled=True
    )
    dwq = jnp.sum(dwq.reshape(seats, depth, held, 3, wide).astype(F32), 1)
    dwq = dwq.transpose(1, 2, 0, 3).reshape(held, 3 * width)
    gain1_grad = jnp.sum(dwq * qkv_weight.astype(F32), -1)
    qkv_grad = dwq * gain1

    near = (xz0.astype(F32) + swap(xw0, 1).astype(F32)).astype(BF16)
    far = (xz1.astype(F32) + swap(xw1, 1).astype(F32)).astype(BF16)
    z1 = near[0].astype(F32)
    for j in range(1, spread):
        z1 = z1 + swap(near[j], inner[j]).astype(F32)
    for j in range(spread):
        z1 = z1 + swap(far[j], across[j]).astype(F32)
    x = tokens.astype(F32)
    inv1 = lax.rsqrt(jnp.mean(x * x, -1, keepdims=True) + EPSILON)
    d_tokens = (
        dy.reshape(tokens.shape)
        + z1
        - x * (inv1 * inv1) * jnp.mean(z1 * x, -1, keepdims=True)
    )
    return (
        output, d_tokens, d_first, gain1_grad, qkv_grad, out_grad_w, gain2_grad, gate_grad, up_grad,
        down_grad,
    )


def solution(mesh):
    rows = P(("seq", "dp"), None)
    acts = P("dp", "seq", None)
    gains = P(("seq", "dp"))
    return jax.shard_map(
        local,
        mesh=mesh,
        in_specs=(acts, acts, acts, P("dp"), gains, rows, rows, gains, rows, rows, rows),
        out_specs=(acts, acts, acts, gains, rows, rows, gains, rows, rows, rows),
        check_vma=False,
    )
```

time: 1950 us -> 554 us (0.28)
  waiting for transfers between devices: 1470 us -> 276 us
  matrix products: 252 us -> 3.6 us
  Pallas kernels: 0 us -> 86.2 us
  blocking collectives: 83.1 us -> 0 us
  starting transfers between devices: 1.89 us -> 66.5 us
  local copies, waits for them, and re-layouts: 75.2 us -> 45.6 us
    reduce_scatter x5 -> x2, waiting for transfers between devices: 910 us -> 50 us  [the longest x1 50 us: local(): lax.psum_scatter(d_wout.reshape(devices, held, width), every, scatter_dim...]
    all_gather x11 -> x2, waiting for transfers between devices: 387 us -> 0.02 us  [the longest x1 0.02 us: local(): tail = lax.all_gather(both_outer(tail), 'dp', axis=0)]
    dot_general x63 -> x2, matrix products: 252 us -> 3.6 us  [the longest x1 2.59 us: dot_tn(): lax.dot_general(a, b, (((0,), (0,)), ((), ())), preferred_element_type=F32)]
    ppermute x0 -> x23, waiting for transfers between devices: none -> 111 us  [swap(): return lax.ppermute(value, 'seq', [(i, i ^ mask) for i in range(seats)])]
    unnamed x28 -> x6, waiting for transfers between devices: 169 us -> 66.4 us
    pallas_call x0 -> x3, Pallas kernels: none -> 86.2 us  [the longest x1 40.7 us: feed_forward(): pl.pallas_call(ff_kernel, grid_spec=pltpu.PrefetchScalarGridSpec(num_scal...]
    unnamed x2 -> x0, blocking collectives: 83.1 us -> none
    all_to_all x0 -> x8, waiting for transfers between devices: none -> 48.6 us  [the longest x1 23.1 us: local(): wqkv = lax.all_to_all(wqkv, every, split_axis=0, concat_axis=0, tiled=True)]
  transfers between devices with their start and end apart: 22 -> 36, of which waited for: 19 -> 15; matrix products, arithmetic and copies ran while one was open for 14% -> 17% of each run, Pallas kernels for 0% -> 8%
where the time goes in v1:
time: 554 us; the launch traced here: 545 us
  waiting for transfers between devices  276 us (50%)
  Pallas kernels  86.2 us (16%)
  starting transfers between devices  66.5 us (12%)
  other arithmetic  53 us (10%)
  local copies, waits for them, and re-layouts  45.6 us (8%)
  between operations  14.7 us (3%)
    ppermute x23, waiting for transfers between devices, swap(): return lax.ppermute(value, 'seq', [(i, i ^ mask) for i in range(seats)])  111 us
    unnamed x6, waiting for transfers between devices  66.4 us
    reduce_scatter x1, waiting for transfers between devices, local(): lax.psum_scatter(d_wout.reshape(devices, held, width), every, scatter_dim...  50 us
    pallas_call x1, Pallas kernels, feed_forward(): pl.pallas_call(ff_kernel, grid_spec=pltpu.PrefetchScalarGridSpec(num_scal...  40.7 us
    ppermute x23, starting transfers between devices, swap(): return lax.ppermute(value, 'seq', [(i, i ^ mask) for i in range(seats)])  33.6 us
    pallas_call x1, Pallas kernels, attn_bwd(): pl.pallas_call(functools.partial(attn_bwd_kernel, order), grid=(micro,),...  24.5 us
    all_to_all x1, waiting for transfers between devices, local(): wqkv = lax.all_to_all(wqkv, every, split_axis=0, concat_axis=0, tiled=True)  23.1 us
    pallas_call x1, Pallas kernels, attn_fwd(): pl.pallas_call(functools.partial(attn_fwd_kernel, order), grid=(micro,),...  20.9 us
  transfers between devices with their start and end apart: 36, of which 15 were waited for; matrix products, arithmetic and copies ran while one was open for 17% of the time, Pallas kernels for 8%

profile of v1, /device:TPU:0, one launch (start us, length us, event | category | flops | bytes accessed | tf_op | source)
XLA Modules:
  0.0 545.2 jit_solution(9443402819156774206)
XLA Ops:
  9.1 3.0 collective-permute-start.8
  12.1 6.0 %collective-permute-done.8 = bf16[120,1024]{1,0:T(8,128)(2,1)S(1)} collective-permute-done((bf16[120,1024]{1,0:T(8,128)(2,1)S(1)}, bf16[120,1024]{1,0:T(8,128)(2,1)S(1)}, u32[]{:S(2)}, u32[]{:S(2)}) %collective-permute-start.8) | collective-permute-done | bytes 245792 | tf_op jit(solution)/shard_map/ppermute | solution.py:452
  22.9 3.5 all-to-all-start.3
  31.4 11.9 %all-to-all-done.3 = bf16[4,32,1408]{2,1,0:T(8,128)(2,1)S(1)} async-done(((bf16[4,32,1408]{2,1,0:T(8,128)(2,1)}), bf16[4,32,1408]{2,1,0:T(8,128)(2,1)S(1)}, u32[]{:S(2)}, u32[]{:S(2)}) %all-to-all-start.3) | async-done | bytes 360480 | tf_op jit(solution)/shard_map/all_to_all | solution.py:486
  43.4 3.9 all-to-all-start.1
  47.3 2.1 collective-permute-start.11
  51.9 15.1 %collective-permute-done.4 = bf16[3,128,1024]{2,1,0:T(8,128)(2,1)} collective-permute-done((bf16[3,128,1024]{2,1,0:T(8,128)(2,1)S(1)}, bf16[3,128,1024]{2,1,0:T(8,128)(2,1)}, u32[]{:S(2)}, u32[]{:S(2)}) %collective-permute-start.4) | collective-permute-done | bytes 786464 | tf_op jit(solution)/shard_map/ppermute | solution.py:452
  67.0 2.7 pad_maximum_fusion.3.xa1
  69.7 2.4 all-to-all-done.1.v1_ref
  73.2 6.3 %all-to-all-start = ((bf16[32,32,384]{2,1,0:T(8,128)(2,1)}), bf16[32,32,384]{2,1,0:T(8,128)(2,1)S(1)}, u32[]{:S(2)}, u32[]{:S(2)}) async-start(bf16[32,32,384]{2,1,0:T(8,128)(2,1)} %bitcast.8), calls=%async_computation | async-start | bytes 1572864 | tf_op jit(solution)/shard_map/all_to_all | solution.py:475
  79.6 2.2 maximum_select_fusion.1
  84.6 23.1 %all-to-all-done = bf16[32,32,384]{2,1,0:T(8,128)(2,1)S(1)} async-done(((bf16[32,32,384]{2,1,0:T(8,128)(2,1)}), bf16[32,32,384]{2,1,0:T(8,128)(2,1)S(1)}, u32[]{:S(2)}, u32[]{:S(2)}) %all-to-all-start) | async-done | bytes 786464 | tf_op jit(solution)/shard_map/all_to_all | solution.py:475
  108.6 20.9 %attn_fwd.1 = (bf16[3,1024,384]{2,1,0:T(8,128)(2,1)}, f32[3,128,1024]{2,1,0:T(8,128)}, bf16[4,3,512,128]{3,2,1,0:T(8,128)(2,1)}, f32[3,2,1024]{2,1,0:T(2,128)}, f32[3,1024,128]{2,1,0:T(8,128)}) custom-call(s32[1]{0:T(128)} %bitcast.seat_ref, s32[3]{0:T(128)} %len_ref.3, bf16[2,3,128,1024]{3,2,1,0:T(8,128)(2,1)} %copy-done.11, ...), custom_call_target="tpu_custom_call" | custom-call | flops 5637144576 | bytes 18874368 | tf_op jit(solution)/shard_map/attn_fwd/pallas_call | solution.py:145
  129.5 4.4 all-to-all-start.2
  135.6 2.0 collective-permute-start.9
  137.7 24.6 %collective-permute-done.9 = bf16[2,1,1,4,32,1024]{5,4,3,0,2,1:T(8,128)(2,1)S(1)} collective-permute-done((bf16[2,1,1,4,32,1024]{5,4,3,0,2,1:T(8,128)(2,1)S(1)}, bf16[2,1,1,4,32,1024]{5,4,3,0,2,1:T(8,128)(2,1)S(1)}, u32[]{:S(2)}, u32[]{:S(2)}) %collective-permute-start.9) | collective-permute-done | bytes 524320 | tf_op jit(solution)/shard_map/ppermute | solution.py:452
  163.8 7.1 %collective-permute-start.10 = (bf16[2,2,1,4,32,1024]{5,4,3,0,2,1:T(8,128)(2,1)}, bf16[2,2,1,4,32,1024]{5,4,3,0,2,1:T(8,128)(2,1)S(1)}, u32[]{:S(2)}, u32[]{:S(2)}) collective-permute-start(bf16[2,2,1,4,32,1024]{5,4,3,0,2,1:T(8,128)(2,1)} %pad_maximum_fusion.4), channel_id=1, source_target_pairs={{0,4},{4,0},{8,12},{12,8},{16,20},{20,16},{24,28},{28,24},{1,5},{5... | collective-permute-start | bytes 3145736 | tf_op jit(solution)/shard_map/ppermute | solution.py:452
  170.9 8.4 %collective-permute-done.2 = bf16[3,128,1024]{2,1,0:T(8,128)(2,1)} collective-permute-done((bf16[3,128,1024]{2,1,0:T(8,128)(2,1)S(1)}, bf16[3,128,1024]{2,1,0:T(8,128)(2,1)}, u32[]{:S(2)}, u32[]{:S(2)}) %collective-permute-start.2) | collective-permute-done | bytes 786464 | tf_op jit(solution)/shard_map/ppermute | solution.py:452
  179.3 2.4 pad_maximum_fusion.2.ga
  181.7 3.3 collective-permute-start.3
  188.2 2.1 slice.99
  194.0 40.7 %feed_forward.1 = (bf16[2,384,1024]{2,1,0:T(8,128)(2,1)}, bf16[2,384,1024]{2,1,0:T(8,128)(2,1)}, bf16[2,384,1024]{2,1,0:T(8,128)(2,1)}, bf16[2,384,1024]{2,1,0:T...) custom-call(s32[1]{0:T(128)} %bitcast.seat_ref, ...), custom_call_target="tpu_custom_call" | custom-call | flops 24964497408 | bytes 34603008 | tf_op jit(solution)/shard_map/feed_forward/pallas_call | solution.py:384
  236.0 4.3 pad_maximum_fusion
  242.3 2.1 add_convert_fusion.2
  252.2 13.9 %collective-permute-done.15 = bf16[384,1024]{1,0:T(8,128)(2,1)} collective-permute-done((bf16[384,1024]{1,0:T(8,128)(2,1)}, bf16[384,1024]{1,0:T(8,128)(2,1)}, u32[]{:S(2)}, u32[]{:S(2)}) %collective-permute-start.15) | collective-permute-done | bytes 786464 | tf_op jit(solution)/shard_map/ppermute | solution.py:452
  267.9 14.0 %collective-permute-done.13 = bf16[384,1024]{1,0:T(8,128)(2,1)} collective-permute-done((bf16[384,1024]{1,0:T(8,128)(2,1)}, bf16[384,1024]{1,0:T(8,128)(2,1)}, u32[]{:S(2)}, u32[]{:S(2)}) %collective-permute-start.13) | collective-permute-done | bytes 786464 | tf_op jit(solution)/shard_map/ppermute | solution.py:452
  281.8 3.4 fusion.6
  287.4 3.6 all-to-all-start.4
  291.0 66.3 %all-reduce.5.cloned.1.call-done = bf16[4,2,4,32,1408]{4,3,0,2,1:T(8,128)(2,1)} async-done(((bf16[4,2,4,32,1408]{4,3,0,2,1:T(8,128)(2,1)}), bf16[4,2,4,32,1408]{4,3,0,2,1:T(8,128)(2,1)}) %all-reduce.5.cloned.1.call-update) | async-done | bytes 2883600
  363.3 24.5 %attn_bwd.1 = (bf16[8,3,128,128]{3,2,1,0:T(8,128)(2,1)}, bf16[2,3,128,1024]{3,2,1,0:T(8,128)(2,1)}, bf16[2,3,128,1024]{3,2,1,0:T(8,128)(2,1)}, bf16[2,3,128,1024...) custom-call(s32[1]{0:T(128)} %bitcast.seat_ref, s32[3]{0:T(128)} %len_ref.3, ...), custom_call_target="tpu_custom_call" | custom-call | flops 12884901888 | bytes 31457280 | tf_op jit(solution)/shard_map/attn_bwd/pallas_call | solution.py:271
  388.0 2.7 fusion.10
  390.6 3.5 all-to-all-start.7
  394.1 2.6 convolution_convert_fusion
  397.3 3.9 all-to-all-done.7
  401.1 3.5 all-to-all-start.5
  407.7 13.5 %collective-permute-done.22 = bf16[88,1024]{1,0:T(8,128)(2,1)S(1)} collective-permute-done((bf16[88,1024]{1,0:T(8,128)(2,1)S(1)}, bf16[88,1024]{1,0:T(8,128)(2,1)S(1)}, u32[]{:S(2)}, u32[]{:S(2)}) %collective-permute-start.22) | collective-permute-done | bytes 180256 | tf_op jit(solution)/shard_map/ppermute | solution.py:452
  426.0 3.6 all-to-all-start.6
  429.6 2.6 add_convert_fusion.1
  434.9 2.1 add_convert_fusion
  443.4 3.0 copy.80
  446.5 3.0 copy.89
  449.5 7.2 %all-to-all-done.6 = bf16[32,32,384]{2,1,0:T(8,128)(2,1)} async-done(((bf16[32,32,384]{2,1,0:T(8,128)(2,1)}), bf16[32,32,384]{2,1,0:T(8,128)(2,1)}, u32[]{:S(2)}, u32[]{:S(2)}) %all-to-all-start.6) | async-done | bytes 786464 | tf_op jit(solution)/shard_map/all_to_all | solution.py:577
  456.7 3.4 reshape.351
  460.1 3.0 reduce_sum.67
  466.0 15.2 %collective-permute-done.19 = bf16[3,128,1024]{2,1,0:T(8,128)(2,1)} collective-permute-done((bf16[3,128,1024]{2,1,0:T(8,128)(2,1)}, bf16[3,128,1024]{2,1,0:T(8,128)(2,1)}, u32[]{:S(2)}, u32[]{:S(2)}) %collective-permute-start.19) | collective-permute-done | bytes 786464 | tf_op jit(solution)/shard_map/ppermute | solution.py:452
  481.3 2.3 fusion
  483.6 3.4 fusion.2
  487.0 50.0 %reduce-scatter.6.cloned.1.call-done = bf16[1,32,1024]{2,1,0:T(8,128)(2,1)} async-done(((bf16[32,32,1024]{2,1,0:T(8,128)(2,1)}), bf16[1,32,1024]{2,1,0:T(8,128)(2,1)}) %reduce-scatter.6.cloned.1.call-update) | async-done | bytes 65552 | tf_op jit(solution)/shard_map/reduce_scatter | solution.py:568
  (186 shorter events, 71.9 us)
Async XLA Ops:
  7.2 11.8 %copy-start = (bf16[3,128,1024]{2,1,0:T(8,128)(2,1)S(1)}, bf16[3,128,1024]{2,1,0:T(8,128)(2,1)}, u32[]{:S(2)}) copy-start(bf16[3,128,1024]{2,1,0:T(8,128)(2,1)} %param.11) | copy-start | bytes 2359300
  7.2 13.5 %copy-start.31 = (bf16[32]{0:T(256)(128)(2,1)S(1)}, bf16[32]{0:T(256)(128)(2,1)}, u32[]{:S(2)}) copy-start(bf16[32]{0:T(256)(128)(2,1)} %param.18) | copy-start | bytes 196
  7.2 13.5 %copy-start.26 = (bf16[32,2816]{1,0:T(8,128)(2,1)S(1)}, bf16[32,2816]{1,0:T(8,128)(2,1)}, u32[]{:S(2)}) copy-start(bf16[32,2816]{1,0:T(8,128)(2,1)} %param.19) | copy-start | bytes 540676
  7.2 13.5 %copy-start.28 = (bf16[32,2816]{1,0:T(8,128)(2,1)S(1)}, bf16[32,2816]{1,0:T(8,128)(2,1)}, u32[]{:S(2)}) copy-start(bf16[32,2816]{1,0:T(8,128)(2,1)} %param.20) | copy-start | bytes 540676
  7.2 127.2 %all-gather.3.cloned.1.call-start = ((), (), s32[]{:S(2)}) async-start(), calls=%async_computation.10 | async-start | bytes 2457600 | tf_op jit(solution)/shard_map/all_gather | solution.py:501
  9.1 8.9 %collective-permute-start.8 = (bf16[120,1024]{1,0:T(8,128)(2,1)S(1)}, bf16[120,1024]{1,0:T(8,128)(2,1)S(1)}, u32[]{:S(2)}, u32[]{:S(2)}) collective-permute-start(bf16[120,1024]{1,0:T(8,128)(2,1)S(1)} %constant_dynamic-update-slice_fusion), channel_id=1, source_target_pairs={{0,16},{4,20},{8,24},{12,28},{16,0},{20,4},{24,8},{28,12},{1,17},{... | collective-permute-start | bytes 737288 | tf_op jit(solution)/shard_map/ppermute | solution.py:452
  19.0 31.6 %collective-permute-start = (bf16[3,128,1024]{2,1,0:T(8,128)(2,1)S(1)}, bf16[3,128,1024]{2,1,0:T(8,128)(2,1)}, u32[]{:S(2)}, u32[]{:S(2)}) collective-permute-start(bf16[3,128,1024]{2,1,0:T(8,128)(2,1)S(1)} %copy-done), channel_id=1, source_target_pairs={{0,8},{4,12},{8,0},{12,4},{16,24},{20,28},{24,16},{28,20},{1,9},{5... | collective-permute-start | bytes 2359304 | tf_op jit(solution)/shard_map/ppermute | solution.py:452
  21.3 8.6 %copy-start.18 = (bf16[3,128,1024]{2,1,0:T(8,128)(2,1)S(1)}, bf16[3,128,1024]{2,1,0:T(8,128)(2,1)}, u32[]{:S(2)}) copy-start(bf16[3,128,1024]{2,1,0:T(8,128)(2,1)} %param.12) | copy-start | bytes 2359300
  22.9 20.4 %all-to-all-start.3 = ((bf16[4,32,1408]{2,1,0:T(8,128)(2,1)}), bf16[4,32,1408]{2,1,0:T(8,128)(2,1)S(1)}, u32[]{:S(2)}, u32[]{:S(2)}) async-start(bf16[4,32,1408]{2,1,0:T(8,128)(2,1)} %pad_maximum_fusion.5), calls=%async_computation.3 | async-start | bytes 720896 | tf_op jit(solution)/shard_map/all_to_all | solution.py:486
  26.4 40.5 %collective-permute-start.4 = (bf16[3,128,1024]{2,1,0:T(8,128)(2,1)S(1)}, bf16[3,128,1024]{2,1,0:T(8,128)(2,1)}, u32[]{:S(2)}, u32[]{:S(2)}) collective-permute-start(bf16[3,128,1024]{2,1,0:T(8,128)(2,1)S(1)} %copy-done), channel_id=1, source_target_pairs={{0,16},{4,20},{8,24},{12,28},{16,0},{20,4},{24,8},{28,12},{1,17},{... | collective-permute-start | bytes 2359304 | tf_op jit(solution)/shard_map/ppermute | solution.py:452
  28.0 39.0 %collective-permute-start.5 = (bf16[3,128,1024]{2,1,0:T(8,128)(2,1)S(1)}, bf16[3,128,1024]{2,1,0:T(8,128)(2,1)}, u32[]{:S(2)}, u32[]{:S(2)}) collective-permute-start(bf16[3,128,1024]{2,1,0:T(8,128)(2,1)S(1)} %copy-done), channel_id=1, source_target_pairs={{0,24},{4,28},{8,16},{12,20},{16,8},{20,12},{24,0},{28,4},{1,25},{... | collective-permute-start | bytes 2359304 | tf_op jit(solution)/shard_map/ppermute | solution.py:452
  30.2 17.1 %copy-start.32 = (bf16[32]{0:T(256)(128)(2,1)S(1)}, bf16[32]{0:T(256)(128)(2,1)}, u32[]{:S(2)}) copy-start(bf16[32]{0:T(256)(128)(2,1)} %param.15) | copy-start | bytes 196
  30.3 19.2 %copy-start.22 = (bf16[32,3072]{1,0:T(8,128)(2,1)S(1)}, bf16[32,3072]{1,0:T(8,128)(2,1)}, u32[]{:S(2)}) copy-start(bf16[32,3072]{1,0:T(8,128)(2,1)} %param.16) | copy-start | bytes 589828
  43.4 28.7 %all-to-all-start.1 = ((bf16[8,3,128,128]{3,2,1,0:T(8,128)(2,1)}), bf16[8,3,128,128]{3,2,1,0:T(8,128)(2,1)S(1)}, u32[]{:S(2)}, u32[]{:S(2)}) async-start(bf16[8,3,128,128]{3,2,1,0:T(8,128)(2,1)} %bitcast.11), calls=%async_computation.1 | async-start | bytes 1572864 | tf_op jit(solution)/shard_map/all_to_all | solution.py:479
  47.3 32.3 %collective-permute-start.11 = (bf16[4,32,1408]{2,1,0:T(8,128)(2,1)S(1)}, bf16[4,32,1408]{2,1,0:T(8,128)(2,1)}, u32[]{:S(2)}, u32[]{:S(2)}) collective-permute-start(bf16[4,32,1408]{2,1,0:T(8,128)(2,1)S(1)} %all-to-all-done.3), channel_id=1, source_target_pairs={{0,16},{4,20},{8,24},{12,28},{16,0},{20,4},{24,8},{28,12},{1,17},{... | collective-permute-start | bytes 1081352 | tf_op jit(solution)/shard_map/ppermute | solution.py:452
  51.8 17.9 %copy-start.11 = (bf16[2,3,128,1024]{3,2,1,0:T(8,128)(2,1)}, bf16[2,3,128,1024]{3,2,1,0:T(8,128)(2,1)S(1)}, u32[]{:S(2)}) copy-start(bf16[2,3,128,1024]{3,2,1,0:T(8,128)(2,1)S(1)} %pad_maximum_fusion.1.xa0.xa) | copy-start | bytes 4718596
  51.8 55.9 %collective-permute-start.1 = (bf16[2,3,128,1024]{3,2,1,0:T(8,128)(2,1)S(1)}, bf16[2,3,128,1024]{3,2,1,0:T(8,128)(2,1)}, u32[]{:S(2)}, u32[]{:S(2)}) collective-permute-start(bf16[2,3,128,1024]{3,2,1,0:T(8,128)(2,1)S(1)} %pad_maximum_fusion.1.xa0.xa), channel_id=1, source_target_pairs={{0,4},{4,0},{8,12},{12,8},{16,20},{20,16},{24,28},{28,24},{1,5},{5... | collective-permute-start | bytes 4718600 | tf_op jit(solution)/shard_map/ppermute | solution.py:452
  69.7 38.1 %collective-permute-start.6 = (bf16[2,3,128,1024]{3,2,1,0:T(8,128)(2,1)}, bf16[2,3,128,1024]{3,2,1,0:T(8,128)(2,1)}, u32[]{:S(2)}, u32[]{:S(2)}) collective-permute-start(bf16[2,3,128,1024]{3,2,1,0:T(8,128)(2,1)} %pad_maximum_fusion.3.xa1), channel_id=1, source_target_pairs={{0,4},{4,0},{8,12},{12,8},{16,20},{20,16},{24,28},{28,24},{1,5},{5... | collective-permute-start | bytes 4718600 | tf_op jit(solution)/shard_map/ppermute | solution.py:452
  73.2 34.5 %all-to-all-start = ((bf16[32,32,384]{2,1,0:T(8,128)(2,1)}), bf16[32,32,384]{2,1,0:T(8,128)(2,1)S(1)}, u32[]{:S(2)}, u32[]{:S(2)}) async-start(bf16[32,32,384]{2,1,0:T(8,128)(2,1)} %bitcast.8), calls=%async_computation | async-start | bytes 1572864 | tf_op jit(solution)/shard_map/all_to_all | solution.py:475
  79.6 108.6 %all-gather.5.cloned.1.call-start = ((), (), s32[]{:S(2)}) async-start(), calls=%async_computation.11 | async-start | bytes 3604480 | tf_op jit(solution)/shard_map/all_gather | solution.py:494
  129.5 55.4 %all-to-all-start.2 = ((bf16[4,3,512,128]{3,2,1,0:T(8,128)(2,1)}), bf16[4,3,512,128]{3,2,1,0:T(8,128)(2,1)}, u32[]{:S(2)}, u32[]{:S(2)}) async-start(bf16[4,3,512,128]{3,2,1,0:T(8,128)(2,1)} %get-tuple-element.30), calls=%async_computation.2 | async-start | bytes 3145728 | tf_op jit(solution)/shard_map/all_to_all | solution.py:519
  133.9 223.5 %all-reduce.5.cloned.1.call-start = ((), (), s32[]{:S(2)}) async-start(), calls=%async_computation.14 | async-start | bytes 5767168
  135.6 26.7 %collective-permute-start.9 = (bf16[2,1,1,4,32,1024]{5,4,3,0,2,1:T(8,128)(2,1)S(1)}, bf16[2,1,1,4,32,1024]{5,4,3,0,2,1:T(8,128)(2,1)S(1)}, u32[]{:S(2)}, u32[]{:S(2)}) collective-permute-start(bf16[2,1,1,4,32,1024]{5,4,3,0,2,1:T(8,128)(2,1)S(1)} %get-tuple-element.84), channel_id=1, source_target_pairs={{0,8},{4,12},{8,0},{12,4},{16,24},{20,28},{24,16},{28,20},{1,9},{5... | collective-permute-start | bytes 1572872 | tf_op jit(solution)/shard_map/ppermute | solution.py:452
  137.6 41.7 %collective-permute-start.2 = (bf16[3,128,1024]{2,1,0:T(8,128)(2,1)S(1)}, bf16[3,128,1024]{2,1,0:T(8,128)(2,1)}, u32[]{:S(2)}, u32[]{:S(2)}) collective-permute-start(bf16[3,128,1024]{2,1,0:T(8,128)(2,1)S(1)} %copy-done.9), channel_id=1, source_target_pairs={{0,8},{4,12},{8,0},{12,4},{16,24},{20,28},{24,16},{28,20},{1,9},{5... | collective-permute-start | bytes 2359304 | tf_op jit(solution)/shard_map/ppermute | solution.py:452
  163.8 22.6 %collective-permute-start.10 = (bf16[2,2,1,4,32,1024]{5,4,3,0,2,1:T(8,128)(2,1)}, bf16[2,2,1,4,32,1024]{5,4,3,0,2,1:T(8,128)(2,1)S(1)}, u32[]{:S(2)}, u32[]{:S(2)}) collective-permute-start(bf16[2,2,1,4,32,1024]{5,4,3,0,2,1:T(8,128)(2,1)} %pad_maximum_fusion.4), channel_id=1, source_target_pairs={{0,4},{4,0},{8,12},{12,8},{16,20},{20,16},{24,28},{28,24},{1,5},{5... | collective-permute-start | bytes 3145736 | tf_op jit(solution)/shard_map/ppermute | solution.py:452
  181.7 12.3 %collective-permute-start.3 = (bf16[2,3,128,1024]{3,2,1,0:T(8,128)(2,1)}, bf16[2,3,128,1024]{3,2,1,0:T(8,128)(2,1)}, u32[]{:S(2)}, u32[]{:S(2)}) collective-permute-start(bf16[2,3,128,1024]{3,2,1,0:T(8,128)(2,1)} %pad_maximum_fusion.2.ga), channel_id=1, source_target_pairs={{0,4},{4,0},{8,12},{12,8},{16,20},{20,16},{24,28},{28,24},{1,5},{5... | collective-permute-start | bytes 4718600 | tf_op jit(solution)/shard_map/ppermute | solution.py:452
  184.9 9.0 %collective-permute-start.7 = (bf16[4,3,512,128]{3,2,1,0:T(8,128)(2,1)}, bf16[4,3,512,128]{3,2,1,0:T(8,128)(2,1)}, u32[]{:S(2)}, u32[]{:S(2)}) collective-permute-start(bf16[4,3,512,128]{3,2,1,0:T(8,128)(2,1)} %all-to-all-done.2.oa_lo.oa_hi), channel_id=1, source_target_pairs={{0,4},{4,0},{8,12},{12,8},{16,20},{20,16},{24,28},{28,24},{1,5},{5... | collective-permute-start | bytes 4718600 | tf_op jit(solution)/shard_map/ppermute | solution.py:452
  234.7 5.8 %collective-permute-start.14 = (bf16[2,384,1024]{2,1,0:T(8,128)(2,1)}, bf16[2,384,1024]{2,1,0:T(8,128)(2,1)S(1)}, u32[]{:S(2)}, u32[]{:S(2)}) collective-permute-start(bf16[2,384,1024]{2,1,0:T(8,128)(2,1)} %get-tuple-element.35), channel_id=1, source_target_pairs={{0,4},{4,0},{8,12},{12,8},{16,20},{20,16},{24,28},{28,24},{1,5},{5... | collective-permute-start | bytes 4718600 | tf_op jit(solution)/shard_map/ppermute | solution.py:452
  240.4 164.3 %reduce-scatter.8.cloned.1.call-start = ((), (), s32[]{:S(2)}) async-start(), calls=%async_computation.13 | async-start | bytes 1802240 | tf_op jit(solution)/shard_map/reduce_scatter | solution.py:547
  240.4 4.9 collective-permute-start.12
  245.4 20.7 %collective-permute-start.15 = (bf16[384,1024]{1,0:T(8,128)(2,1)}, bf16[384,1024]{1,0:T(8,128)(2,1)}, u32[]{:S(2)}, u32[]{:S(2)}) collective-permute-start(bf16[384,1024]{1,0:T(8,128)(2,1)} %slice_bitcast_fusion.4), channel_id=1, source_target_pairs={{0,8},{4,12},{8,0},{12,4},{16,24},{20,28},{24,16},{28,20},{1,9},{5... | collective-permute-start | bytes 2359304 | tf_op jit(solution)/shard_map/ppermute | solution.py:452
  248.9 32.9 %collective-permute-start.13 = (bf16[384,1024]{1,0:T(8,128)(2,1)}, bf16[384,1024]{1,0:T(8,128)(2,1)}, u32[]{:S(2)}, u32[]{:S(2)}) collective-permute-start(bf16[384,1024]{1,0:T(8,128)(2,1)} %slice_bitcast_fusion.6), channel_id=1, source_target_pairs={{0,8},{4,12},{8,0},{12,4},{16,24},{20,28},{24,16},{28,20},{1,9},{5... | collective-permute-start | bytes 2359304 | tf_op jit(solution)/shard_map/ppermute | solution.py:452
  250.9 15.2 %copy-start.2 = (f32[384,1024]{1,0:T(8,128)S(1)}, f32[384,1024]{1,0:T(8,128)}, u32[]{:S(2)}) copy-start(f32[384,1024]{1,0:T(8,128)} %get-tuple-element.31) | copy-start | bytes 4718596
  266.1 15.7 %copy-start.3 = (f32[384,1024]{1,0:T(8,128)S(1)}, f32[384,1024]{1,0:T(8,128)}, u32[]{:S(2)}) copy-start(f32[384,1024]{1,0:T(8,128)} %get-tuple-element.31) | copy-start | bytes 4718596
  266.1 15.7 %copy-start.5 = (bf16[2,384,1024]{2,1,0:T(8,128)(2,1)S(1)}, bf16[2,384,1024]{2,1,0:T(8,128)(2,1)}, u32[]{:S(2)}) copy-start(bf16[2,384,1024]{2,1,0:T(8,128)(2,1)} %copy-done.4) | copy-start | bytes 4718596
  287.4 75.0 %all-to-all-start.4 = ((bf16[8,3,128,128]{3,2,1,0:T(8,128)(2,1)}), bf16[8,3,128,128]{3,2,1,0:T(8,128)(2,1)S(1)}, u32[]{:S(2)}, u32[]{:S(2)}) async-start(bf16[8,3,128,128]{3,2,1,0:T(8,128)(2,1)} %bitcast.139), calls=%async_computation.4 | async-start | bytes 1572864 | tf_op jit(solution)/shard_map/all_to_all | solution.py:541
  360.8 27.1 %collective-permute-start.21 = (bf16[4,32,1408]{2,1,0:T(8,128)(2,1)S(1)}, bf16[4,32,1408]{2,1,0:T(8,128)(2,1)}, u32[]{:S(2)}, u32[]{:S(2)}) collective-permute-start(bf16[4,32,1408]{2,1,0:T(8,128)(2,1)S(1)} %fusion.23), channel_id=1, source_target_pairs={{0,16},{4,20},{8,24},{12,28},{16,0},{20,4},{24,8},{28,12},{1,17},{... | collective-permute-start | bytes 1081352 | tf_op jit(solution)/shard_map/ppermute | solution.py:452
  387.9 41.7 %collective-permute-start.16 = (bf16[2,3,128,1024]{3,2,1,0:T(8,128)(2,1)}, bf16[2,3,128,1024]{3,2,1,0:T(8,128)(2,1)}, u32[]{:S(2)}, u32[]{:S(2)}) collective-permute-start(bf16[2,3,128,1024]{3,2,1,0:T(8,128)(2,1)} %get-tuple-element.41), channel_id=1, source_target_pairs={{0,4},{4,0},{8,12},{12,8},{16,20},{20,16},{24,28},{28,24},{1,5},{5... | collective-permute-start | bytes 4718600 | tf_op jit(solution)/shard_map/ppermute | solution.py:452
  390.6 10.5 %all-to-all-start.7 = ((bf16[4,32,1408]{2,1,0:T(8,128)(2,1)}), bf16[4,32,1408]{2,1,0:T(8,128)(2,1)S(1)}, u32[]{:S(2)}, u32[]{:S(2)}) async-start(bf16[4,32,1408]{2,1,0:T(8,128)(2,1)} %fusion.10), calls=%async_computation.8 | async-start | bytes 720896 | tf_op jit(solution)/shard_map/all_to_all | solution.py:557
  394.1 142.8 %reduce-scatter.6.cloned.1.call-start = ((), (), s32[]{:S(2)}) async-start(), calls=%async_computation.12 | async-start | bytes 2162688 | tf_op jit(solution)/shard_map/reduce_scatter | solution.py:568
  396.8 38.1 %collective-permute-start.18 = (bf16[2,3,128,1024]{3,2,1,0:T(8,128)(2,1)}, bf16[2,3,128,1024]{3,2,1,0:T(8,128)(2,1)}, u32[]{:S(2)}, u32[]{:S(2)}) collective-permute-start(bf16[2,3,128,1024]{3,2,1,0:T(8,128)(2,1)} %get-tuple-element.43), channel_id=1, source_target_pairs={{0,4},{4,0},{8,12},{12,8},{16,20},{20,16},{24,28},{28,24},{1,5},{5... | collective-permute-start | bytes 4718600 | tf_op jit(solution)/shard_map/ppermute | solution.py:452
  401.1 24.8 %all-to-all-start.5 = ((bf16[8,3,128,128]{3,2,1,0:T(8,128)(2,1)}), bf16[8,3,128,128]{3,2,1,0:T(8,128)(2,1)S(1)}, u32[]{:S(2)}, u32[]{:S(2)}) async-start(bf16[8,3,128,128]{3,2,1,0:T(8,128)(2,1)} %get-tuple-element.44), calls=%async_computation.5 | async-start | bytes 1572864 | tf_op jit(solution)/shard_map/all_to_all | solution.py:575
  405.8 15.5 %collective-permute-start.22 = (bf16[88,1024]{1,0:T(8,128)(2,1)S(1)}, bf16[88,1024]{1,0:T(8,128)(2,1)S(1)}, u32[]{:S(2)}, u32[]{:S(2)}) collective-permute-start(bf16[88,1024]{1,0:T(8,128)(2,1)S(1)} %select_bitcast_fusion), channel_id=1, source_target_pairs={{0,16},{4,20},{8,24},{12,28},{16,0},{20,4},{24,8},{28,12},{1,17},{... | collective-permute-start | bytes 540680 | tf_op jit(solution)/shard_map/ppermute | solution.py:452
  426.0 30.7 %all-to-all-start.6 = ((bf16[32,32,384]{2,1,0:T(8,128)(2,1)}), bf16[32,32,384]{2,1,0:T(8,128)(2,1)}, u32[]{:S(2)}, u32[]{:S(2)}) async-start(bf16[32,32,384]{2,1,0:T(8,128)(2,1)} %bitcast.170), calls=%async_computation.6 | async-start | bytes 1572864 | tf_op jit(solution)/shard_map/all_to_all | solution.py:577
  433.1 32.9 %collective-permute-start.17 = (bf16[3,128,1024]{2,1,0:T(8,128)(2,1)}, bf16[3,128,1024]{2,1,0:T(8,128)(2,1)}, u32[]{:S(2)}, u32[]{:S(2)}) collective-permute-start(bf16[3,128,1024]{2,1,0:T(8,128)(2,1)} %slice_bitcast_fusion.2), channel_id=1, source_target_pairs={{0,8},{4,12},{8,0},{12,4},{16,24},{20,28},{24,16},{28,20},{1,9},{5... | collective-permute-start | bytes 2359304 | tf_op jit(solution)/shard_map/ppermute | solution.py:452
  438.3 43.0 %collective-permute-start.19 = (bf16[3,128,1024]{2,1,0:T(8,128)(2,1)}, bf16[3,128,1024]{2,1,0:T(8,128)(2,1)}, u32[]{:S(2)}, u32[]{:S(2)}) collective-permute-start(bf16[3,128,1024]{2,1,0:T(8,128)(2,1)} %get-tuple-element.86), channel_id=1, source_target_pairs={{0,16},{4,20},{8,24},{12,28},{16,0},{20,4},{24,8},{28,12},{1,17},{... | collective-permute-start | bytes 2359304 | tf_op jit(solution)/shard_map/ppermute | solution.py:452
  439.8 41.5 %collective-permute-start.20 = (bf16[3,128,1024]{2,1,0:T(8,128)(2,1)}, bf16[3,128,1024]{2,1,0:T(8,128)(2,1)}, u32[]{:S(2)}, u32[]{:S(2)}) collective-permute-start(bf16[3,128,1024]{2,1,0:T(8,128)(2,1)} %get-tuple-element.87), channel_id=1, source_target_pairs={{0,24},{4,28},{8,16},{12,20},{16,8},{20,12},{24,0},{28,4},{1,25},{... | collective-permute-start | bytes 2359304 | tf_op jit(solution)/shard_map/ppermute | solution.py:452
  463.2 18.1 %copy-start.1 = (bf16[3,128,1024]{2,1,0:T(8,128)(2,1)S(1)}, bf16[3,128,1024]{2,1,0:T(8,128)(2,1)}, u32[]{:S(2)}) copy-start(bf16[3,128,1024]{2,1,0:T(8,128)(2,1)} %param.11) | copy-start | bytes 2359300
  (23 other events, 65.6 us)
Sparse Core Ops, SparseCore 0:
  19.1 45.0 all-gather.2
  82.0 65.0 all-gather.4
  240.5 116.7 all-reduce.4
  359.5 32.2 reduce-scatter.7
  396.9 140.0 reduce-scatter.5
